TPU v7x, 128 devices: a whole 4x4x4 slice. The times are simulated.
128 devices in a mesh: ep: 32 (over z, y, core), tp: 4 (over x).
Axes of the slice: x: 4, y: 4, z: 4, core: 2. Of those that a mesh axis runs over, the one named last changes fastest.
Arguments:
- hidden_in: bfloat16 [4096, 5120], P('ep', 'tp'), may hold values from -12 to 12
- out_grad: bfloat16 [4096, 5120], P('ep', 'tp'), may hold values from -6 to 6
- norm_gain: float32 [5120], P('tp'), may hold values from 0.5 to 1.5
- router_weight: float32 [5120, 32], P('tp'), may hold values from -0.078125 to 0.078125
- route_ids: int32 [4096, 8], P('ep'), may hold values from 0 to 31, all different within a row; in each aligned block of 128 rows (0 to 127, 128 to 255, ...) at most 36 rows name the same one
- expert_gate: bfloat16 [32, 5120, 768], P('ep', 'tp'), may hold values from -0.078125 to 0.078125
- expert_up: bfloat16 [32, 5120, 768], P('ep', 'tp'), may hold values from -0.078125 to 0.078125
- expert_down: bfloat16 [32, 768, 5120], P('ep', None, 'tp'), may hold values from -0.21875 to 0.21875
- shared_gate: bfloat16 [5120, 768], P('tp', 'ep'), may hold values from -0.078125 to 0.078125
- shared_up: bfloat16 [5120, 768], P('tp', 'ep'), may hold values from -0.078125 to 0.078125
- shared_down: bfloat16 [768, 5120], P('ep', 'tp'), may hold values from -0.21875 to 0.21875
- dense_gate: bfloat16 [4096, 6144], P(None, 'ep'), may hold values from -6 to 6
- dense_up: bfloat16 [4096, 6144], P(None, 'ep'), may hold values from -6 to 6
- dense_down: bfloat16 [6144, 5120], P('ep', 'tp'), may hold values from -0.078125 to 0.078125
Outputs:
- grad_gate2: bfloat16 [4096, 6144], P('tp', 'ep')
- grad_up2: bfloat16 [4096, 6144], P('tp', 'ep')
- grad_dense_down: bfloat16 [6144, 5120], P('ep', 'tp')
- grad_expert_gate: bfloat16 [32, 5120, 768], P('ep', 'tp')
- grad_expert_up: bfloat16 [32, 5120, 768], P('ep', 'tp')
- grad_expert_down: bfloat16 [32, 768, 5120], P('ep', None, 'tp')
- grad_shared_gate: bfloat16 [5120, 768], P('tp', 'ep')
- grad_shared_up: bfloat16 [5120, 768], P('tp', 'ep')
- grad_shared_down: bfloat16 [768, 5120], P('ep', 'tp')
- grad_router: float32 [5120, 32], P('tp')
Inputs may be any that keep to these rules, and one draw needn't show every extreme that they name: `route_ids`: each row names 8 different experts. Among the rows of one index of ep (128 consecutive tokens) no expert is named more than 36 times, a bound that some block reaches. A pair (t, k) takes slot number p of its expert's slots from that index, where p counts the earlier pairs of the same index and expert in the order of t, then k.
All inputs are finite; a program needn't handle non-finite values.
Results may differ from a plain program's by a relative error of at most 0.035.
Values may be sent and summed in bfloat16 or wider, within the bound.
No kernel may reach another device: no remote copies, remote signals or barrier semaphores. Data moves between devices by JAX's collectives and lax.ppermute only.
A program may use at most 128 MiB of HBM per device.

v0:
```python
import jax
import jax.numpy as jnp
from jax import lax
from jax.sharding import PartitionSpec as P

EXPERTS = 32
TOP = 8
CAP = 36


EPSILON = 1e-05
ROUTE_SCALE = 2.5


def gate_grads(hidden_cot, gate_value, up_value):
    sigma = jax.nn.sigmoid(gate_value)
    gate_cot = (hidden_cot * up_value * sigma * (1.0 + gate_value * (1.0 - sigma))).astype(
        jnp.bfloat16
    )
    up_cot = (hidden_cot * gate_value * sigma).astype(jnp.bfloat16)
    return (gate_cot, up_cot)


def local(
    hidden_in,
    out_grad,
    norm_gain,
    router_weight,
    route_ids,
    expert_gate,
    expert_up,
    expert_down,
    shared_gate,
    shared_up,
    shared_down,
    dense_gate,
    dense_up,
    dense_down,
):
    highest = lax.Precision.HIGHEST
    tok_rows, quarter = hidden_in.shape
    feature_count = quarter * lax.axis_size("tp")
    wide_in = hidden_in.astype(jnp.float32)
    square_sum = lax.psum(jnp.sum(wide_in * wide_in, axis=1, keepdims=True), "tp")
    inv_rms = lax.rsqrt(square_sum / feature_count + EPSILON)
    normed = (wide_in * inv_rms * norm_gain).astype(jnp.bfloat16)
    logits = lax.psum(jnp.dot(normed.astype(jnp.float32), router_weight, precision=highest), "tp")
    scores = jax.nn.sigmoid(logits)
    picks = (route_ids[:, :, None] == jnp.arange(EXPERTS, dtype=jnp.int32)[None, None, :]).astype(
        jnp.float32
    )
    chosen = jnp.sum(picks * scores[:, None, :], axis=2)
    chosen_total = jnp.sum(chosen, axis=1, keepdims=True)
    route_weight = ROUTE_SCALE * chosen / chosen_total
    weight_low = route_weight.astype(jnp.bfloat16)
    pair_count = tok_rows * TOP
    flat_ids = route_ids.reshape(pair_count)
    member = (flat_ids[:, None] == jnp.arange(EXPERTS, dtype=jnp.int32)[None, :]).astype(jnp.int32)
    before = jnp.cumsum(member, axis=0) - member
    position = jnp.sum(before * member, axis=1)
    slot_index = flat_ids * CAP + position
    source = (
        jnp.full((EXPERTS * CAP,), pair_count, jnp.int32)
        .at[slot_index]
        .set(jnp.arange(pair_count, dtype=jnp.int32))
    )
    pair_row = source // TOP
    normed_pad = jnp.concatenate([normed, jnp.zeros((1, quarter), jnp.bfloat16)], axis=0)
    grad_pad = jnp.concatenate([out_grad, jnp.zeros((1, quarter), jnp.bfloat16)], axis=0)
    weight_pad = jnp.concatenate([weight_low.reshape(-1), jnp.zeros((1,), jnp.bfloat16)], axis=0)
    send_in = normed_pad[pair_row].reshape(EXPERTS, CAP, quarter)
    send_grad = grad_pad[pair_row].reshape(EXPERTS, CAP, quarter)
    send_weight = weight_pad[source].reshape(EXPERTS, CAP)
    rows_in, rows_grad, rows_weight = (
        lax.all_to_all(send_in, "ep", split_axis=0, concat_axis=1, tiled=True),
        lax.all_to_all(send_grad, "ep", split_axis=0, concat_axis=1, tiled=True),
        lax.all_to_all(send_weight, "ep", split_axis=0, concat_axis=1, tiled=True),
    )
    gate_part = jnp.einsum("erd,edf->erf", rows_in, expert_gate, preferred_element_type=jnp.float32)
    up_part = jnp.einsum("erd,edf->erf", rows_in, expert_up, preferred_element_type=jnp.float32)
    gate_value, up_value = (
        lax.psum(gate_part.astype(jnp.bfloat16), "tp").astype(jnp.float32),
        lax.psum(up_part.astype(jnp.bfloat16), "tp").astype(jnp.float32),
    )
    hidden = (jax.nn.silu(gate_value) * up_value).astype(jnp.bfloat16)
    out_rows = jnp.einsum(
        "erf,efd->erd", hidden, expert_down, preferred_element_type=jnp.float32
    ).astype(jnp.bfloat16)
    out_cot = (rows_weight.astype(jnp.float32)[:, :, None] * rows_grad.astype(jnp.float32)).astype(
        jnp.bfloat16
    )
    hidden_part = jnp.einsum(
        "erd,efd->erf", out_cot, expert_down, preferred_element_type=jnp.float32
    )
    hidden_cot = lax.psum(hidden_part.astype(jnp.bfloat16), "tp").astype(jnp.float32)
    gate_cot, up_cot = gate_grads(hidden_cot, gate_value, up_value)
    grad_expert_down = jnp.einsum(
        "erf,erd->efd", hidden, out_cot, preferred_element_type=jnp.float32
    ).astype(jnp.bfloat16)
    grad_expert_gate = jnp.einsum(
        "erd,erf->edf", rows_in, gate_cot, preferred_element_type=jnp.float32
    ).astype(jnp.bfloat16)
    grad_expert_up = jnp.einsum(
        "erd,erf->edf", rows_in, up_cot, preferred_element_type=jnp.float32
    ).astype(jnp.bfloat16)
    back_rows = (
        jnp.einsum("erf,edf->erd", gate_cot, expert_gate, preferred_element_type=jnp.float32)
        + jnp.einsum("erf,edf->erd", up_cot, expert_up, preferred_element_type=jnp.float32)
    ).astype(jnp.bfloat16)
    returned_rows, returned_out = (
        lax.all_to_all(back_rows, "ep", split_axis=1, concat_axis=0, tiled=True),
        lax.all_to_all(out_rows, "ep", split_axis=1, concat_axis=0, tiled=True),
    )
    returned_inner = jnp.sum(
        send_grad.astype(jnp.float32) * returned_out.astype(jnp.float32), axis=2
    ).astype(jnp.bfloat16)
    flat_back = returned_rows.reshape(EXPERTS * CAP, quarter)
    routed_cot = jnp.sum(
        flat_back[slot_index].astype(jnp.float32).reshape(tok_rows, TOP, quarter), axis=1
    )
    inner_pairs = (
        returned_inner.reshape(EXPERTS * CAP)[slot_index].astype(jnp.float32).reshape(tok_rows, TOP)
    )
    weight_cot = lax.psum(inner_pairs.astype(jnp.bfloat16), "tp").astype(jnp.float32)
    chosen_cot = ROUTE_SCALE * (
        weight_cot / chosen_total
        - jnp.sum(weight_cot * chosen, axis=1, keepdims=True) / (chosen_total * chosen_total)
    )
    score_cot = jnp.sum(picks * chosen_cot[:, :, None], axis=1)
    logit_cot = score_cot * scores * (1.0 - scores)
    router_part = jnp.dot(normed.astype(jnp.float32).T, logit_cot, precision=highest)
    grad_router = lax.psum(router_part.astype(jnp.bfloat16), "ep").astype(jnp.float32)
    router_cot = jnp.dot(logit_cot, router_weight.T, precision=highest)
    gate_whole, up_whole, down_whole = (
        lax.all_gather(shared_gate, "ep", axis=1, tiled=True),
        lax.all_gather(shared_up, "ep", axis=1, tiled=True),
        lax.all_gather(shared_down, "ep", axis=0, tiled=True),
    )
    gate_s_part = jnp.dot(normed, gate_whole, preferred_element_type=jnp.float32)
    up_s_part = jnp.dot(normed, up_whole, preferred_element_type=jnp.float32)
    gate_s, up_s = (
        lax.psum(gate_s_part.astype(jnp.bfloat16), "tp").astype(jnp.float32),
        lax.psum(up_s_part.astype(jnp.bfloat16), "tp").astype(jnp.float32),
    )
    hid_s = (jax.nn.silu(gate_s) * up_s).astype(jnp.bfloat16)
    hid_cot_s = lax.psum(
        jnp.dot(out_grad, down_whole.T, preferred_element_type=jnp.float32).astype(jnp.bfloat16),
        "tp",
    ).astype(jnp.float32)
    gate_cot_s, up_cot_s = gate_grads(hid_cot_s, gate_s, up_s)
    shared_gate_term = jnp.dot(normed.T, gate_cot_s, preferred_element_type=jnp.float32)
    shared_up_term = jnp.dot(normed.T, up_cot_s, preferred_element_type=jnp.float32)
    shared_down_term = jnp.dot(hid_s.T, out_grad, preferred_element_type=jnp.float32)
    summed_gate, summed_up, summed_down = (
        lax.psum_scatter(
            shared_gate_term.astype(jnp.bfloat16), "ep", scatter_dimension=1, tiled=True
        ).astype(jnp.float32),
        lax.psum_scatter(
            shared_up_term.astype(jnp.bfloat16), "ep", scatter_dimension=1, tiled=True
        ).astype(jnp.float32),
        lax.psum_scatter(
            shared_down_term.astype(jnp.bfloat16), "ep", scatter_dimension=0, tiled=True
        ).astype(jnp.float32),
    )
    grad_shared_gate = summed_gate.astype(jnp.bfloat16)
    grad_shared_up = summed_up.astype(jnp.bfloat16)
    grad_shared_down = summed_down.astype(jnp.bfloat16)
    shared_cot = jnp.dot(gate_cot_s, gate_whole.T, preferred_element_type=jnp.float32) + jnp.dot(
        up_cot_s, up_whole.T, preferred_element_type=jnp.float32
    )
    normed_cot = routed_cot + shared_cot + router_cot
    scaled = normed_cot * norm_gain
    inner_sum = lax.psum(jnp.sum(scaled * wide_in, axis=1, keepdims=True), "tp")
    input_cot = inv_rms * scaled - wide_in * (inv_rms * inv_rms * inv_rms) * (
        inner_sum / feature_count
    )
    dense_cot = (out_grad.astype(jnp.float32) + input_cot).astype(jnp.bfloat16)
    cot_whole = lax.all_gather(dense_cot, "ep", axis=0, tiled=True)
    gate_two = dense_gate.astype(jnp.float32)
    hidden2 = (jax.nn.silu(gate_two) * dense_up.astype(jnp.float32)).astype(jnp.bfloat16)
    grad_dense_down = jnp.dot(hidden2.T, cot_whole, preferred_element_type=jnp.float32).astype(
        jnp.bfloat16
    )
    share_rows = cot_whole.shape[0] // lax.axis_size("tp")
    hidden2_cot = lax.psum_scatter(
        jnp.dot(cot_whole, dense_down.T, preferred_element_type=jnp.float32).astype(jnp.bfloat16),
        "tp",
        scatter_dimension=0,
        tiled=True,
    ).astype(jnp.float32)
    first_row = lax.axis_index("tp") * share_rows
    gate_mine = lax.dynamic_slice_in_dim(dense_gate, first_row, share_rows, 0).astype(jnp.float32)
    up_mine = lax.dynamic_slice_in_dim(dense_up, first_row, share_rows, 0).astype(jnp.float32)
    grad_gate2, grad_up2 = gate_grads(hidden2_cot, gate_mine, up_mine)
    return (
        grad_gate2,
        grad_up2,
        grad_dense_down,
        grad_expert_gate,
        grad_expert_up,
        grad_expert_down,
        grad_shared_gate,
        grad_shared_up,
        grad_shared_down,
        grad_router,
    )


def solution(mesh):
    in_specs = (
        P("ep", "tp"),
        P("ep", "tp"),
        P("tp"),
        P("tp", None),
        P("ep", None),
        P("ep", "tp", None),
        P("ep", "tp", None),
        P("ep", None, "tp"),
        P("tp", "ep"),
        P("tp", "ep"),
        P("ep", "tp"),
        P(None, "ep"),
        P(None, "ep"),
        P("ep", "tp"),
    )
    out_specs = (
        P("tp", "ep"),
        P("tp", "ep"),
        P("ep", "tp"),
        P("ep", "tp", None),
        P("ep", "tp", None),
        P("ep", None, "tp"),
        P("tp", "ep"),
        P("tp", "ep"),
        P("ep", "tp"),
        P("tp", None),
    )
    return jax.shard_map(local, mesh=mesh, in_specs=in_specs, out_specs=out_specs, check_vma=False)
```

profile of v0, /device:TPU:0, one launch (start us, length us, event | category | flops | bytes accessed | tf_op | source)
XLA Modules:
  0.0 985.6 jit_solution(9463463383330336537)
XLA Ops:
  9.8 9.0 reduce-window.6
  20.3 10.6 %psum.77 = f32[128,1]{0,1:T(1,128)S(1)} all-reduce(f32[128,1]{0,1:T(1,128)S(1)} %bitcast.130), channel_id=1, replica_groups=mesh['ep'=32,'tp'=4] {'tp'}, use_global_device_ids=true, to_apply=%region_1.0 | all-reduce | flops 128 | bytes 1024 | tf_op jit(solution)/shard_map/psum | solution.py:44
  32.0 1.3 fusion.100
  33.3 14.3 %psum.78 = f32[128,32]{0,1:T(8,128)S(1)} all-reduce(f32[128,32]{0,1:T(8,128)S(1)} %fusion.100), channel_id=1, replica_groups=mesh['ep'=32,'tp'=4] {'tp'}, use_global_device_ids=true, to_apply=%region_2.0 | all-reduce | flops 4096 | bytes 32768 | tf_op jit(solution)/shard_map/psum | solution.py:47
  48.8 4.3 scatter_custom_fusion
  53.2 7.3 gather_fusion
  61.2 8.3 all-to-all-start
  69.6 5.2 gather_fusion.2
  74.7 5.3 reshape.262
  80.0 7.6 all-to-all-start.2
  88.5 5.2 gather_fusion.1
  93.7 5.3 reshape.260
  98.9 32.9 %all-to-all-done.2 = bf16[32,36,1280]{2,1,0:T(8,128)(2,1)} async-done(((bf16[32,36,1280]{2,1,0:T(8,128)(2,1)}), bf16[32,36,1280]{2,1,0:T(8,128)(2,1)}, u32[]{:S(2)}, u32[]{:S(2)}) %all-to-all-start.2) | async-done | bytes 2949152 | tf_op jit(solution)/shard_map/all_to_all | solution.py:75
  131.8 4.8 all-to-all-start.1
  137.8 5.3 reshape.263
  143.1 40.0 %all-to-all-done.1 = bf16[32,36,1280]{2,1,0:T(8,128)(2,1)} async-done(((bf16[32,36,1280]{2,1,0:T(8,128)(2,1)}), bf16[32,36,1280]{2,1,0:T(8,128)(2,1)}, u32[]{:S(2)}, u32[]{:S(2)}) %all-to-all-start.1) | async-done | bytes 2949152 | tf_op jit(solution)/shard_map/all_to_all | solution.py:76
  183.0 5.7 reshape.271
  188.7 6.3 fusion.21
  195.0 3.7 fusion.20
  198.7 3.8 fusion.19
  202.5 3.0 convolution_convert_fusion.15
  205.5 3.0 convolution_convert_fusion.13
  208.5 15.6 %all-gather.7.cloned.1.call-done = bf16[1280,768]{0,1:T(8,128)(2,1)} async-done(((bf16[1280,24]{0,1:T(8,128)(2,1)}), bf16[1280,768]{0,1:T(8,128)(2,1)}) %all-gather.7.cloned.1.call-update) | async-done | bytes 1966096 | tf_op jit(solution)/shard_map/all_gather | solution.py:136
  224.1 3.0 convolution_convert_fusion.14
  227.2 120.7 %all-reduce.8.cloned.1.call-done = (bf16[1,1152,768]{2,1,0:T(8,128)(2,1)}, bf16[1,1152,768]{2,1,0:T(8,128)(2,1)}, bf16[1,1152,768]{2,1,0:T(8,128)(2,1)}, bf16[12...) async-done(((bf16[1,1152,768]{2,1,0:T(8,128)(2,1)}, bf16[1,1152,768]{2,1,0:T(8,128)(2,1)}, bf16[1,1152,768]{2,1,0:T(8,128)(2,1)}, ...) | async-done | bytes 5898256 | tf_op jit(solution)/shard_map/psum | solution.py:83
  347.9 5.1 fusion.1
  353.0 19.4 %copy.74 = bf16[1,1152,1280]{2,0,1:T(2,128)(2,1)} copy(bf16[1,1152,1280]{2,1,0:T(8,128)(2,1)S(1)} %fusion.1) | data formatting | bytes 5898240 | tf_op jit(solution)/shard_map/convert_element_type | solution.py:88
  372.9 18.1 %reduce.7 = bf16[1152,1280]{1,0:T(8,128)(2,1)S(1)} reduce(bf16[1152,1,1280]{2,1,0:T(2,128)(2,1)} %bitcast.119, bf16[]{:T(256)} %broadcast.206), dimensions={1}, to_apply=%bitcast.115.reduce_sub_computation | reduce | bytes 5898242
  391.0 2.5 reshape.336
  393.5 7.7 all-to-all-start.4
  401.2 4.3 fusion.6
  405.5 1.2 copy-done.14
  406.7 2.5 fusion.28
  409.3 3.1 fusion.2
  412.4 19.4 %copy.75 = bf16[1,1152,1280]{2,0,1:T(2,128)(2,1)} copy(bf16[1,1152,1280]{2,1,0:T(8,128)(2,1)S(1)} %fusion.2) | data formatting | bytes 5898240 | tf_op jit(solution)/shard_map/convert_element_type | solution.py:109
  431.8 19.8 %reduce.6 = bf16[1152,1280]{1,0:T(8,128)(2,1)} reduce(bf16[1152,1,1280]{2,1,0:T(2,128)(2,1)} %bitcast.120, bf16[]{:T(256)} %broadcast.206), dimensions={1}, to_apply=%bitcast.116.reduce_sub_computation | reduce | bytes 5898242
  451.6 7.0 reshape.334
  458.6 7.8 all-to-all-start.3
  466.6 3.1 fusion.94
  469.8 18.7 %reshape.337 = bf16[1152,1,1280]{2,1,0:T(2,128)(2,1)} reshape(bf16[32,2,23040]{2,1,0:T(2,128)(2,1)} %copy-done.3) | data formatting | bytes 5898240
  488.4 3.5 fusion.3
  491.9 6.8 gather_fusion.4
  498.9 8.6 psum.85
  507.6 18.6 %reshape.335 = bf16[1152,1,1280]{2,1,0:T(2,128)(2,1)} reshape(bf16[32,2,23040]{2,1,0:T(2,128)(2,1)} %all-to-all-done.3) | data formatting | bytes 5898240
  526.2 3.1 copy.73
  529.3 5.5 gather_fusion.3
  534.8 3.6 convert_reduce_fusion
  540.4 8.9 psum.86
  551.3 56.2 %all-gather.11.cloned.1.call-done = bf16[4096,1280]{1,0:T(8,128)(2,1)} async-done(((bf16[128,1280]{1,0:T(8,128)(2,1)}), bf16[4096,1280]{1,0:T(8,128)(2,1)}) %all-gather.11.cloned.1.call-update) | async-done | bytes 10485776 | tf_op jit(solution)/shard_map/all_gather | solution.py:178
  607.6 8.7 convolution_convert_fusion.1
  616.3 2.1 convolution_convert_fusion.10
  618.5 2.0 convolution_convert_fusion.8
  620.8 3.2 convolution_convert_fusion.9
  624.0 6.3 fusion.23
  630.3 5.6 fusion.22
  636.0 7.3 fusion.24
  643.2 63.8 %all-reduce.6.cloned.1.call-done = bf16[1280,32]{0,1:T(8,128)(2,1)} async-done(((bf16[1280,32]{0,1:T(8,128)(2,1)}), bf16[1280,32]{0,1:T(8,128)(2,1)}) %all-reduce.6.cloned.1.call-update) | async-done | bytes 81936 | tf_op jit(solution)/shard_map/psum | solution.py:132
  707.0 1.6 convert_element_type.332
  708.6 8.1 convolution_convert_fusion.11
  716.7 18.1 %reduce-scatter.5.cloned.1.call-done = bf16[1024,192]{0,1:T(8,128)(2,1)} async-done(((bf16[4096,192]{0,1:T(8,128)(2,1)}), bf16[1024,192]{0,1:T(8,128)(2,1)}) %reduce-scatter.5.cloned.1.call-update) | async-done | bytes 393232 | tf_op jit(solution)/shard_map/reduce_scatter | solution.py:185
  734.8 2.4 fusion.51
  737.2 79.4 %reduce-scatter.7.cloned.1.call-done = bf16[1280,24]{0,1:T(8,128)(2,1)} async-done(((bf16[1280,768]{0,1:T(8,128)(2,1)}), bf16[1280,24]{0,1:T(8,128)(2,1)}) %reduce-scatter.7.cloned.1.call-update) | async-done | bytes 61456 | tf_op jit(solution)/shard_map/reduce_scatter | solution.py:155
  816.6 80.8 %reduce-scatter.11.cloned.1.call-done = bf16[24,1280]{1,0:T(8,128)(2,1)} async-done(((bf16[768,1280]{1,0:T(8,128)(2,1)}), bf16[24,1280]{1,0:T(8,128)(2,1)}) %reduce-scatter.11.cloned.1.call-update) | async-done | bytes 61456 | tf_op jit(solution)/shard_map/reduce_scatter | solution.py:161
  897.4 81.1 %reduce-scatter.9.cloned.1.call-done = bf16[1280,24]{0,1:T(8,128)(2,1)} async-done(((bf16[1280,768]{0,1:T(8,128)(2,1)}), bf16[1280,24]{0,1:T(8,128)(2,1)}) %reduce-scatter.9.cloned.1.call-update) | async-done | bytes 61456 | tf_op jit(solution)/shard_map/reduce_scatter | solution.py:158
  (128 shorter events, 14.4 us)
Async XLA Ops:
  7.2 191.6 %copy-start = (bf16[1,768,1280]{2,1,0:T(8,128)(2,1)S(1)}, bf16[1,768,1280]{2,1,0:T(8,128)(2,1)}, u32[]{:S(2)}) copy-start(bf16[1,768,1280]{2,1,0:T(8,128)(2,1)} %param.21) | copy-start | bytes 5898244
  7.2 195.3 %all-gather.5.cloned.1.call-start = ((), (), s32[]{:S(2)}) async-start(), calls=%async_computation.9 | async-start | bytes 2027520 | tf_op jit(solution)/shard_map/all_gather | solution.py:137
  61.2 18.8 %all-to-all-start = ((bf16[32,1,36]{2,1,0:T(2,128)(2,1)}), bf16[32,1,36]{2,1,0:T(2,128)(2,1)S(1)}, u32[]{:S(2)}, u32[]{:S(2)}) async-start(bf16[32,1,36]{2,1,0:T(2,128)(2,1)} %all_to_all.19), calls=%async_computation | async-start | bytes 32768 | tf_op jit(solution)/shard_map/all_to_all | solution.py:77
  80.0 8.4 copy-start.6
  80.0 51.8 %all-to-all-start.2 = ((bf16[32,36,1280]{2,1,0:T(8,128)(2,1)}), bf16[32,36,1280]{2,1,0:T(8,128)(2,1)}, u32[]{:S(2)}, u32[]{:S(2)}) async-start(bf16[32,36,1280]{2,1,0:T(8,128)(2,1)} %reshape.262), calls=%async_computation.2 | async-start | bytes 6553600 | tf_op jit(solution)/shard_map/all_to_all | solution.py:75
  87.7 117.9 %all-gather.9.cloned.1.call-start = ((), (), s32[]{:S(2)}) async-start(), calls=%async_computation.11 | async-start | bytes 2027520 | tf_op jit(solution)/shard_map/all_gather | solution.py:135
  131.8 51.2 %all-to-all-start.1 = ((bf16[32,36,1280]{2,1,0:T(8,128)(2,1)}), bf16[32,36,1280]{2,1,0:T(8,128)(2,1)}, u32[]{:S(2)}, u32[]{:S(2)}) async-start(bf16[32,36,1280]{2,1,0:T(8,128)(2,1)} %reshape.260), calls=%async_computation.1 | async-start | bytes 6553600 | tf_op jit(solution)/shard_map/all_to_all | solution.py:76
  136.7 87.5 %all-gather.7.cloned.1.call-start = ((), (), s32[]{:S(2)}) async-start(), calls=%async_computation.10 | async-start | bytes 2027520 | tf_op jit(solution)/shard_map/all_gather | solution.py:136
  137.4 210.5 %all-reduce.8.cloned.1.call-start = ((), (), s32[]{:S(2)}) async-start(), calls=%async_computation.18 | async-start | bytes 11796480 | tf_op jit(solution)/shard_map/psum | solution.py:83
  188.7 6.3 copy-start.8
  188.7 6.3 copy-start.23
  188.7 10.0 %slice-start = ((s8[5898240]{0:T(1024)(128)(4,1)}), s8[4194304]{0:T(1024)(128)(4,1)S(1)}, s32[]{:S(2)}) async-start(s8[5898240]{0:T(1024)(128)(4,1)} %bitcast.123), calls=%async_computation.19 | async-start | bytes 8388608
  195.0 3.7 slice-start.1
  393.5 65.1 %all-to-all-start.4 = ((bf16[32,2,23040]{2,1,0:T(2,128)(2,1)}), bf16[32,2,23040]{2,1,0:T(2,128)(2,1)S(1)}, u32[]{:S(2)}, u32[]{:S(2)}) async-start(bf16[32,2,23040]{2,1,0:T(2,128)(2,1)} %reshape.336), calls=%async_computation.4 | async-start | bytes 5898240 | tf_op jit(solution)/shard_map/all_to_all | solution.py:112
  401.2 5.5 copy-start.22
  405.4 1.2 copy-start.14
  406.7 2.5 copy-start.11
  406.7 2.5 copy-start.13
  406.7 2.6 copy-start.24
  458.6 8.0 copy-start.15
  458.6 8.0 copy-start.3
  458.6 49.0 %all-to-all-start.3 = ((bf16[32,2,23040]{2,1,0:T(2,128)(2,1)}), bf16[32,2,23040]{2,1,0:T(2,128)(2,1)}, u32[]{:S(2)}, u32[]{:S(2)}) async-start(bf16[32,2,23040]{2,1,0:T(2,128)(2,1)} %reshape.334), calls=%async_computation.3 | async-start | bytes 5898240 | tf_op jit(solution)/shard_map/all_to_all | solution.py:111
  466.4 141.2 %all-gather.11.cloned.1.call-start = ((), (), s32[]{:S(2)}) async-start(), calls=%async_computation.12 | async-start | bytes 10813440 | tf_op jit(solution)/shard_map/all_gather | solution.py:178
  469.7 18.7 %copy-start.2 = (bf16[1152,1280]{1,0:T(8,128)(2,1)S(1)}, bf16[1152,1280]{1,0:T(8,128)(2,1)}, u32[]{:S(2)}) copy-start(bf16[1152,1280]{1,0:T(8,128)(2,1)} %gather_fusion.1) | copy-start | bytes 8847364
  488.4 19.1 %copy-start.20 = (s32[128,8]{0,1:T(8,128)S(1)}, s32[128,8]{0,1:T(8,128)}, u32[]{:S(2)}) copy-start(s32[128,8]{0,1:T(8,128)} %param.18) | copy-start | bytes 12292
  534.8 3.6 copy-start.4
  534.8 3.6 copy-start.16
  534.8 3.6 copy-start.18
  538.5 1.0 copy-start.5
  538.5 1.0 copy-start.17
  538.5 1.0 copy-start.21
  538.5 10.8 %copy-start.7 = (bf16[128,1280]{1,0:T(8,128)(2,1)S(1)}, bf16[128,1280]{1,0:T(8,128)(2,1)}, u32[]{:S(2)}) copy-start(bf16[128,1280]{1,0:T(8,128)(2,1)} %param.15) | copy-start | bytes 983044
  539.5 68.1 %copy-start.25 = (bf16[192,1280]{1,0:T(8,128)(2,1)S(1)}, bf16[192,1280]{1,0:T(8,128)(2,1)}, u32[]{:S(2)}) copy-start(bf16[192,1280]{1,0:T(8,128)(2,1)} %param.27) | copy-start | bytes 1474564
  550.3 156.7 %all-reduce.6.cloned.1.call-start = ((), (), s32[]{:S(2)}) async-start(), calls=%async_computation.17 | async-start | bytes 163840 | tf_op jit(solution)/shard_map/psum | solution.py:132
  551.3 65.0 %copy-start.26 = (bf16[128,768]{1,0:T(8,128)(2,1)S(1)}, bf16[128,768]{1,0:T(8,128)(2,1)}, u32[]{:S(2)}) copy-start(bf16[128,768]{1,0:T(8,128)(2,1)} %get-tuple-element.15) | copy-start | bytes 589828
  551.3 183.5 %reduce-scatter.5.cloned.1.call-start = ((), (), s32[]{:S(2)}) async-start(), calls=%async_computation.13 | async-start | bytes 1966080 | tf_op jit(solution)/shard_map/reduce_scatter | solution.py:185
  616.3 200.4 %reduce-scatter.7.cloned.1.call-start = ((), (), s32[]{:S(2)}) async-start(), calls=%async_computation.14 | async-start | bytes 2027520 | tf_op jit(solution)/shard_map/reduce_scatter | solution.py:155
  618.4 279.0 %reduce-scatter.11.cloned.1.call-start = ((), (), s32[]{:S(2)}) async-start(), calls=%async_computation.16 | async-start | bytes 2027520 | tf_op jit(solution)/shard_map/reduce_scatter | solution.py:161
  620.5 3.5 copy-start.9
  620.5 358.0 %reduce-scatter.9.cloned.1.call-start = ((), (), s32[]{:S(2)}) async-start(), calls=%async_computation.15 | async-start | bytes 2027520 | tf_op jit(solution)/shard_map/reduce_scatter | solution.py:158
  630.3 5.6 copy-start.10
  630.3 5.6 copy-start.12
  636.0 72.6 %copy-start.19 = (bf16[4096,192]{0,1:T(8,128)(2,1)S(1)}, bf16[4096,192]{0,1:T(8,128)(2,1)}, u32[]{:S(2)}) copy-start(bf16[4096,192]{0,1:T(8,128)(2,1)} %param.25) | copy-start | bytes 4718596
  708.6 269.9 %copy-start.1 = (bf16[1,768,1280]{2,1,0:T(8,128)(2,1)S(1)}, bf16[1,768,1280]{2,1,0:T(8,128)(2,1)}, u32[]{:S(2)}) copy-start(bf16[1,768,1280]{2,1,0:T(8,128)(2,1)} %param.21) | copy-start | bytes 5898244
Sparse Core Ops, SparseCore 0:
  10.3 46.2 all-gather.4
  90.8 78.1 all-gather.8
  171.4 52.7 all-gather.6
  227.3 120.4 all-reduce.7
  550.4 57.1 all-gather.10
  611.2 95.6 all-reduce.5
  709.5 25.2 reduce-scatter.4
  739.4 77.1 reduce-scatter.6
  820.8 76.5 reduce-scatter.10
  901.8 76.6 reduce-scatter.8
where the time goes:
time: 994 us; the launch traced here: 986 us
  waiting for transfers between devices  591 us (59%)
  local copies, waits for them, and re-layouts  150 us (15%)
  matrix products  83.6 us (8%)
  other arithmetic  67.3 us (7%)
  blocking collectives  42.4 us (4%)
  starting transfers between devices  37.2 us (4%)
  between operations  14.9 us (1%)
    psum x1, waiting for transfers between devices, local(): lax.psum(up_part.astype(jnp.bfloat16), 'tp').astype(jnp.float32)  121 us
    reduce_scatter x1, waiting for transfers between devices, local(): lax.psum_scatter(shared_up_term.astype(jnp.bfloat16), 'ep', scatter_dimen...  81.1 us
    reduce_scatter x1, waiting for transfers between devices, local(): lax.psum_scatter(shared_down_term.astype(jnp.bfloat16), 'ep', scatter_dim...  80.8 us
    reduce_scatter x1, waiting for transfers between devices, local(): lax.psum_scatter(shared_gate_term.astype(jnp.bfloat16), 'ep', scatter_dim...  79.4 us
    psum x1, waiting for transfers between devices, local(): lax.psum(router_part.astype(jnp.bfloat16), 'ep').astype(jnp.float32)  63.8 us
    all_gather x1, waiting for transfers between devices, local(): cot_whole = lax.all_gather(dense_cot, 'ep', axis=0, tiled=True)  56.2 us
    unnamed x65, local copies, waits for them, and re-layouts  53.1 us
    all_to_all x1, waiting for transfers between devices, local(): lax.all_to_all(send_grad, 'ep', split_axis=0, concat_axis=1, tiled=True)  40 us
  transfers between devices with their start and end apart: 15, of which 10 were waited for; matrix products, arithmetic and copies ran while one was open for 22% of the time, Pallas kernels for 0%

commit v1 on v0

v1 whole, which is shorter than its diff:
```python
import functools

import jax
import jax.numpy as jnp
from jax import lax
from jax.experimental import pallas as pl
from jax.experimental.pallas import tpu as pltpu
from jax.sharding import PartitionSpec as P

EXPERTS = 32
TOP = 8
CAP = 36
SIDE = 4
GROUPS = 8
ROWS = SIDE * CAP

EPSILON = 1e-05
ROUTE_SCALE = 2.5
F32 = jnp.float32
BF16 = jnp.bfloat16
HIGHEST = lax.Precision.HIGHEST
VMEM_BYTES = 50 * 1024 * 1024


def ep_at(z, y, core):
    return ((z % SIDE) * SIDE + y % SIDE) * 2 + core


def ep_pairs(target):
    return [
        (ep_at(z, y, core), target(z, y, core))
        for z in range(SIDE)
        for y in range(SIDE)
        for core in range(2)
    ]


def first_hop(k):
    return ep_pairs(lambda z, y, core: ep_at(z, y + k, 1) if core else ep_at(z + k, y, 0))


def second_hop(k):
    return ep_pairs(lambda z, y, core: ep_at(z + k, y, 1) if core else ep_at(z, y + k, 0))


def swap_second_hop(k):
    return ep_pairs(lambda z, y, core: ep_at(z, y + k, 0) if core else ep_at(z + k, y, 1))


def core_swap():
    return ep_pairs(lambda z, y, core: ep_at(z, y, 1 - core))


def tp_hop(k):
    return [(i, (i + k) % SIDE) for i in range(SIDE)]


def join_kernel(*refs):
    blocks, out = refs[:SIDE], refs[SIDE]
    rows = blocks[0].shape[0]
    for i in range(SIDE):
        out[i * rows : (i + 1) * rows] = blocks[i][...]


def join(blocks):
    rows, width = blocks[0].shape
    return local_call(
        join_kernel,
        jax.ShapeDtypeStruct((SIDE * rows, width), blocks[0].dtype),
        vmem(SIDE),
        0,
        4 * SIDE * rows * width,
    )(*blocks)


def path_gather(block, after=None):
    if after is not None:
        block, unused = lax.optimization_barrier((block, after[0]))
    first = [block] + [lax.ppermute(block, "ep", first_hop(k)) for k in range(1, SIDE)]
    joined = join(first)
    if after is not None:
        joined, *unused = lax.optimization_barrier((joined, *after[1:SIDE]))
    own = [joined] + [lax.ppermute(joined, "ep", second_hop(k)) for k in range(1, SIDE)]
    other = [lax.ppermute(chunk, "ep", core_swap()) for chunk in own]
    return own + other


def ep_sum(value):
    for dz, dy, dcore in ((0, 0, 1), (0, 1, 0), (1, 0, 0), (0, 2, 0), (2, 0, 0)):
        pairs = ep_pairs(lambda z, y, core: ep_at(z ^ dz, y ^ dy, core ^ dcore))
        value = value + lax.ppermute(value, "ep", pairs)
    return value


def tp_sum(value):
    return value + sum(lax.ppermute(value, "tp", tp_hop(k)) for k in range(1, SIDE))


def tp_exchange(parts):
    return lax.all_to_all(parts, "tp", split_axis=0, concat_axis=0, tiled=True)


def tp_scatter(parts):
    return jnp.sum(tp_exchange(parts).astype(F32), axis=0)


def vmem(count):
    return [pl.BlockSpec(memory_space=pltpu.VMEM)] * count


def smem():
    return pl.BlockSpec(memory_space=pltpu.SMEM)


def local_call(body, out_shape, in_specs, flops, moved, scratch=()):
    many = isinstance(out_shape, (list, tuple))
    return pl.pallas_call(
        body,
        out_shape=out_shape,
        in_specs=in_specs,
        out_specs=vmem(len(out_shape)) if many else vmem(1)[0],
        scratch_shapes=list(scratch),
        cost_estimate=pl.CostEstimate(flops=flops, bytes_accessed=moved, transcendentals=0),
        compiler_params=pltpu.CompilerParams(vmem_limit_bytes=VMEM_BYTES),
    )


def nt_dot(left, right):
    return lax.dot_general(left, right, (((1,), (1,)), ((), ())), preferred_element_type=F32)


def dispatch_kernel(scale, slot, *refs):
    if scale:
        inv, gain, *refs = refs
    chunks, out = refs[:GROUPS], refs[GROUPS]
    for g in range(GROUPS):
        tokens = chunks[g].shape[0]
        hit = lax.broadcasted_iota(jnp.int32, (ROWS, tokens), 0) == slot[g]
        pick = jnp.where(hit, 1.0, 0.0).astype(BF16)
        rows = jnp.dot(pick, chunks[g][...], preferred_element_type=F32)
        if scale:
            row_inv = jnp.sum(jnp.where(hit, inv[g], 0.0), axis=1, keepdims=True)
            rows = rows * row_inv * gain[...]
        out[g] = rows.astype(BF16)


def dispatch(slot, chunks, inv=None, gain=None):
    scale = inv is not None
    tokens, width = chunks[0].shape
    extra = (inv, gain) if scale else ()
    return local_call(
        functools.partial(dispatch_kernel, scale),
        jax.ShapeDtypeStruct((GROUPS, ROWS, width), BF16),
        vmem(1 + len(extra) + GROUPS),
        2 * GROUPS * ROWS * tokens * width,
        2 * GROUPS * (tokens + ROWS) * width,
    )(slot, *extra, *chunks)


def back_kernel(cots, weights, *out):
    tile = 256

    def step(n, unused):
        columns = pl.ds(pl.multiple_of(n * tile, tile), tile)
        for k in range(SIDE):
            rows = jnp.dot(cots[k], weights[:, columns], preferred_element_type=F32).astype(BF16)
            out[2 * k][:, columns] = rows[:ROWS]
            out[2 * k + 1][:, columns] = rows[ROWS:]
        return unused

    lax.fori_loop(0, weights.shape[1] // tile, step, 0)


def back_rows_of(cots, weights):
    hidden, width = weights.shape
    return local_call(
        back_kernel,
        [jax.ShapeDtypeStruct((ROWS, width), BF16)] * GROUPS,
        vmem(2),
        2 * GROUPS * ROWS * hidden * width,
        2 * (GROUPS * ROWS * hidden + hidden * width + GROUPS * ROWS * width),
    )(cots, weights)


def act_kernel(weight, gate_ups, cots, cot_out, hidden_out, row_cot, row_inner):
    tile = 32
    width = cots.shape[2]

    def step(n, unused):
        rows = pl.ds(pl.multiple_of(n * tile, tile), tile)

        def total(parts, columns):
            return sum(parts[k, rows, columns].astype(F32) for k in range(SIDE))

        gate = total(gate_ups, slice(0, width))
        up = total(gate_ups, slice(width, 2 * width))
        cot = total(cots, slice(0, width))
        weight_here = weight[rows, :]
        sigma = 1.0 / (1.0 + jnp.exp(-gate))
        silu = gate * sigma
        hidden = silu * up
        row_cot[rows, :] = jnp.sum(cot * hidden, axis=1, keepdims=True)
        cot = cot * weight_here
        gate_cot = cot * up * (sigma + silu * (1.0 - sigma))
        up_cot = cot * silu
        row_inner[rows, :] = jnp.sum(gate_cot * gate + up_cot * up, axis=1, keepdims=True)
        for k in range(SIDE):
            cot_out[k, rows, :width] = gate_cot.astype(BF16)
            cot_out[k, rows, width:] = up_cot.astype(BF16)
            hidden_out[k, rows, :] = (hidden * weight_here).astype(BF16)
        return unused

    lax.fori_loop(0, weight.shape[0] // tile, step, 0)


def act(weight, gate_ups, cots):
    parts, rows, hidden = cots.shape
    return local_call(
        act_kernel,
        [
            jax.ShapeDtypeStruct((parts, rows, 2 * hidden), BF16),
            jax.ShapeDtypeStruct((parts, rows, hidden), BF16),
        ]
        + [jax.ShapeDtypeStruct((rows, 1), F32)] * 2,
        vmem(3),
        40 * rows * hidden,
        48 * rows * hidden,
    )(weight, gate_ups, cots)


def combine_kernel(slots, *refs):
    rows, out, pick = refs[:GROUPS], refs[GROUPS], refs[GROUPS + 1]
    tokens = slots.shape[0]
    tile = 256
    for m in range(GROUPS):
        hit = lax.broadcasted_iota(jnp.int32, (tokens, ROWS), 1) == slots[:, m : m + 1]
        pick[m] = jnp.where(hit, 1.0, 0.0).astype(BF16)

    def step(n, unused):
        columns = pl.ds(pl.multiple_of(n * tile, tile), tile)
        total = jnp.dot(pick[0], rows[0][:, columns], preferred_element_type=F32)
        for m in range(1, GROUPS):
            total = total + jnp.dot(pick[m], rows[m][:, columns], preferred_element_type=F32)
        out[:, columns] = total.astype(BF16)
        return unused

    lax.fori_loop(0, out.shape[1] // tile, step, 0)


def combine(slots, rows):
    tokens, width = slots.shape[0], rows[0].shape[1]
    return local_call(
        combine_kernel,
        jax.ShapeDtypeStruct((tokens, width), BF16),
        vmem(1 + GROUPS),
        2 * GROUPS * ROWS * tokens * width,
        2 * (GROUPS * ROWS + tokens) * width,
        [pltpu.VMEM((GROUPS, tokens, ROWS), BF16)],
    )(slots, *rows)


def shared_kernel(place, w_in, w_out, *refs):
    ins, grads, out = refs[:GROUPS], refs[GROUPS : 2 * GROUPS], refs[2 * GROUPS]
    top, block = w_in.shape[0], out.shape[2]
    for g in range(GROUPS):
        first = nt_dot(w_in[...], ins[g][...]).astype(BF16)
        second = nt_dot(w_out[...], grads[g][...]).astype(BF16)
        for i in range(SIDE):
            at = place[g * SIDE + i]
            out[at, :top] = first[:, i * block : (i + 1) * block]
            out[at, top:] = second[:, i * block : (i + 1) * block]


def shared_partials(place, w_in, w_out, ins, grads):
    tokens, width = ins[0].shape
    hidden = w_in.shape[0] + w_out.shape[0]
    return local_call(
        shared_kernel,
        jax.ShapeDtypeStruct((GROUPS * SIDE, hidden, tokens // SIDE), BF16),
        [smem()] + vmem(2 + 2 * GROUPS),
        2 * GROUPS * tokens * width * hidden,
        4 * GROUPS * tokens * width,
    )(place, w_in, w_out, *ins, *grads)


def shared_grad_kernel(place, cots, gain, *refs):
    ins, grads = refs[:GROUPS], refs[GROUPS : 2 * GROUPS]
    out_in, out_down, sum_in, sum_down = refs[2 * GROUPS :]
    top = out_in.shape[0]
    for g in range(GROUPS):
        cot = jnp.concatenate([cots[place[g * SIDE + i]] for i in range(SIDE)], axis=1)
        first = jnp.dot(cot[:top], ins[g][...], preferred_element_type=F32)
        second = jnp.dot(cot[top:], grads[g][...], preferred_element_type=F32)
        sum_in[...] = first if g == 0 else sum_in[...] + first
        sum_down[...] = second if g == 0 else sum_down[...] + second
    out_in[...] = (sum_in[...] * gain[...]).astype(BF16)
    out_down[...] = sum_down[...].astype(BF16)


def shared_grads(place, cots, gain, ins, grads, top):
    tokens, width = ins[0].shape
    rest = cots.shape[1] - top
    return local_call(
        shared_grad_kernel,
        [jax.ShapeDtypeStruct((top, width), BF16), jax.ShapeDtypeStruct((rest, width), BF16)],
        [smem()] + vmem(2 + 2 * GROUPS),
        2 * GROUPS * tokens * width * (top + rest),
        4 * GROUPS * tokens * width,
        [pltpu.VMEM((top, width), F32), pltpu.VMEM((rest, width), F32)],
    )(place, cots, gain, *ins, *grads)


def dense_hidden_kernel(place, w_down, *refs):
    chunks, out = refs[:GROUPS], refs[GROUPS]
    block = chunks[0].shape[0] // SIDE
    for g in range(GROUPS):
        columns = nt_dot(w_down[...], chunks[g][...]).astype(BF16)
        for i in range(SIDE):
            at = place[g * SIDE + i]
            lane = pl.multiple_of(lax.rem(at, 8) * block, block)
            out[lax.div(at, 8), :, pl.ds(lane, block)] = columns[:, i * block : (i + 1) * block]


def dense_hidden(place, w_down, chunks):
    tokens, width = chunks[0].shape
    hidden = w_down.shape[0]
    return local_call(
        dense_hidden_kernel,
        jax.ShapeDtypeStruct((SIDE, hidden, 2 * tokens), BF16),
        [smem()] + vmem(1 + GROUPS),
        2 * GROUPS * tokens * width * hidden,
        2 * GROUPS * tokens * width,
    )(place, w_down, *chunks)


def dense_grad_kernel(place, hidden, *refs):
    chunks, out, total = refs[:GROUPS], refs[GROUPS], refs[GROUPS + 1]
    block = chunks[0].shape[0] // SIDE
    for g in range(GROUPS):
        left = jnp.concatenate(
            [
                hidden[:, pl.ds(pl.multiple_of(place[g * SIDE + i] * block, block), block)]
                for i in range(SIDE)
            ],
            axis=1,
        )
        term = jnp.dot(left, chunks[g][...], preferred_element_type=F32)
        total[...] = term if g == 0 else total[...] + term
    out[...] = total[...].astype(BF16)


def dense_grad(place, hidden, chunks):
    tokens, width = chunks[0].shape
    units = hidden.shape[0]
    return local_call(
        dense_grad_kernel,
        jax.ShapeDtypeStruct((units, width), BF16),
        [smem()] + vmem(1 + GROUPS),
        2 * GROUPS * tokens * width * units,
        2 * GROUPS * tokens * width,
        [pltpu.VMEM((units, width), F32)],
    )(place, hidden, *chunks)


def gate_grads(hidden_cot, gate_value, up_value):
    sigma = jax.nn.sigmoid(gate_value)
    gate_cot = hidden_cot * up_value * sigma * (1.0 + gate_value * (1.0 - sigma))
    up_cot = hidden_cot * gate_value * sigma
    return (gate_cot, up_cot)


def local(
    hidden_in,
    out_grad,
    norm_gain,
    router_weight,
    route_ids,
    expert_gate,
    expert_up,
    expert_down,
    shared_gate,
    shared_up,
    shared_down,
    dense_gate,
    dense_up,
    dense_down,
):
    tok_rows, quarter = hidden_in.shape
    feature_count = quarter * lax.axis_size("tp")
    ep, tp = lax.axis_index("ep"), lax.axis_index("tp")
    z, y, core = ep // 8, (ep // 2) % SIDE, ep % 2
    w_gate, w_up, w_down = expert_gate[0], expert_up[0], expert_down[0]
    gain = norm_gain[None, :]

    in_chunks = path_gather(hidden_in)
    grad_chunks = path_gather(out_grad, in_chunks)

    g_at = jnp.arange(GROUPS, dtype=jnp.int32)[:, None]
    i_at = jnp.arange(SIDE, dtype=jnp.int32)[None, :]
    j_at = g_at % SIDE
    block_core = (core + g_at // SIDE) % 2
    block_z = jnp.where(block_core == 0, z - i_at, z - j_at) % SIDE
    block_y = jnp.where(block_core == 0, y - j_at, y - i_at) % SIDE
    block_of = ((block_z * SIDE + block_y) * 2 + block_core).reshape(-1)
    to_path = (block_of[:, None] == jnp.arange(EXPERTS, dtype=jnp.int32)[None, :]).astype(F32)

    wide_in = hidden_in.astype(F32)
    square_part = jnp.sum(wide_in * wide_in, axis=1, keepdims=True)
    logit_part = jnp.dot(wide_in * gain, router_weight, precision=HIGHEST)
    stats = tp_sum(jnp.concatenate([logit_part, square_part], axis=1))
    plain_logits = stats[:, :EXPERTS]
    mean_square = stats[:, EXPERTS:] / feature_count + EPSILON
    inv_rms = lax.rsqrt(mean_square)
    rms = mean_square * inv_rms
    normed = (wide_in * inv_rms * gain).astype(BF16)
    scores = jax.nn.sigmoid(plain_logits * inv_rms)
    picks = jnp.any(
        route_ids[:, :, None] == jnp.arange(EXPERTS, dtype=jnp.int32)[None, None, :], axis=1
    ).astype(F32)
    chosen = picks * scores
    chosen_total = jnp.sum(chosen, axis=1, keepdims=True)
    route_weight = ROUTE_SCALE * chosen / chosen_total

    token_line = jnp.arange(tok_rows, dtype=jnp.int32)
    earlier = (token_line[:, None] < token_line[None, :]).astype(F32)
    own_position = jnp.dot(picks.T, earlier, precision=HIGHEST)
    own_position = jnp.where(picks.T > 0.0, own_position, -1.0)
    told = jnp.concatenate(
        [
            own_position[:, None, :],
            route_weight.T[:, None, :],
            jnp.broadcast_to(inv_rms.reshape(1, 1, tok_rows), (EXPERTS, 1, tok_rows)),
        ],
        axis=1,
    )
    told = lax.all_to_all(told, "ep", split_axis=0, concat_axis=0, tiled=True)
    told_path = jnp.dot(to_path, told.reshape(EXPERTS, 3 * tok_rows), precision=HIGHEST)
    told_path = told_path.reshape(GROUPS, SIDE, 3, tok_rows)
    position = told_path[:, :, 0].astype(jnp.int32)
    offset = (CAP * jnp.arange(SIDE, dtype=jnp.int32))[None, :, None]
    slot = jnp.where(position >= 0, position + offset, -1).reshape(GROUPS, 1, SIDE * tok_rows)
    weight_path = told_path[:, :, 1].reshape(GROUPS, 1, SIDE * tok_rows)
    inv_path = told_path[:, :, 2].reshape(GROUPS, 1, SIDE * tok_rows)

    s_line = jnp.arange(2, dtype=jnp.int32)[None, :]
    j_line = jnp.arange(SIDE, dtype=jnp.int32)
    j_col = j_line[:, None]
    return_expert = jnp.where(
        core == 0,
        (z * SIDE + (y + j_col) % SIDE) * 2 + s_line,
        (((z + j_col) % SIDE) * SIDE + y) * 2 + 1 - s_line,
    ).reshape(-1)
    pick_expert = (
        return_expert[:, None] == jnp.arange(EXPERTS, dtype=jnp.int32)[None, :]
    ).astype(F32)
    line_position = jnp.stack(
        [own_position]
        + [lax.ppermute(own_position, "ep", first_hop(k)) for k in range(1, SIDE)]
    )
    position_here = jnp.einsum(
        "ket,me->ktm", line_position, pick_expert, precision=HIGHEST
    ).astype(jnp.int32)
    return_slot = jnp.where(
        position_here >= 0, position_here + (CAP * j_line)[:, None, None], -1
    ).reshape(SIDE * tok_rows, GROUPS)

    w_both = jnp.concatenate([w_gate, w_up], axis=1)
    w_both_t = jnp.concatenate([w_gate.T, w_up.T], axis=0)
    rows_in = dispatch(slot, in_chunks, inv_path, gain).reshape(-1, quarter)
    both_part = jnp.dot(rows_in, w_both, preferred_element_type=F32).astype(BF16)
    rows_grad = dispatch(slot, grad_chunks).reshape(-1, quarter)
    hidden_part = jnp.dot(rows_grad, w_down.T, preferred_element_type=F32).astype(BF16)
    quarter_rows = 2 * ROWS
    both_terms = tp_exchange(both_part.reshape(SIDE, quarter_rows, -1))
    cot_terms = tp_exchange(hidden_part.reshape(SIDE, quarter_rows, -1))
    own_slot = lax.dynamic_slice_in_dim(slot, 2 * tp, 2, 0)
    own_weight = lax.dynamic_slice_in_dim(weight_path, 2 * tp, 2, 0)
    own_hit = jnp.arange(ROWS, dtype=jnp.int32)[None, :, None] == own_slot
    row_weight = jnp.sum(jnp.where(own_hit, own_weight, 0.0), axis=2).reshape(quarter_rows, 1)
    both_cot, hidden, row_cot, row_inner = act(row_weight, both_terms, cot_terms)
    both_cots = tp_exchange(both_cot)
    hidden, unused = lax.optimization_barrier((hidden, both_cots))
    hidden_all = tp_exchange(hidden).reshape(GROUPS * ROWS, -1)
    back = back_rows_of(both_cots, w_both_t)

    returned = []
    for j in range(SIDE):
        own, other = back[j], back[SIDE + j]
        returned.append(own if j == 0 else lax.ppermute(own, "ep", second_hop(-j)))
        returned.append(lax.ppermute(other, "ep", swap_second_hop(-j)))
    summed = combine(return_slot, returned).reshape(SIDE, tok_rows, quarter)
    routed_cot = summed[0].astype(F32)
    for k in range(1, SIDE):
        routed_cot = routed_cot + lax.ppermute(summed[k], "ep", first_hop(-k)).astype(F32)

    units = shared_down.shape[0]
    shared_in = (jnp.concatenate([shared_gate.T, shared_up.T], axis=0).astype(F32) * gain).astype(
        BF16
    )
    shared_out = jnp.concatenate([shared_down, jnp.zeros((8, quarter), BF16)], axis=0)
    late_in, late_grad, unused = lax.optimization_barrier((in_chunks, grad_chunks, hidden_part))
    parts = shared_partials(block_of, shared_in, shared_out, late_in, late_grad)
    inner = parts.shape[1]
    shared_sum = tp_scatter(parts.reshape(SIDE, 8, inner, tok_rows))
    own_inv = lax.dynamic_slice_in_dim(told[:, 2:], 8 * tp, 8, 0)
    gate_s = shared_sum[:, :units] * own_inv
    up_s = shared_sum[:, units : 2 * units] * own_inv
    hid_cot_s = shared_sum[:, 2 * units : 3 * units]
    gate_cot_s, up_cot_s = gate_grads(hid_cot_s, gate_s, up_s)
    cots = jnp.concatenate(
        [
            gate_cot_s * own_inv,
            up_cot_s * own_inv,
            gate_s * jax.nn.sigmoid(gate_s) * up_s,
            jnp.zeros((8, 8, tok_rows), F32),
        ],
        axis=1,
    ).astype(BF16)
    cots_all = tp_exchange(jnp.broadcast_to(cots[None], (SIDE,) + cots.shape))
    grads_in, grads_down = shared_grads(
        block_of, cots_all.reshape(EXPERTS, inner, tok_rows), gain, in_chunks, grad_chunks, 2 * units
    )
    to_owner = cots_all[:, :, : 2 * units].reshape(EXPERTS, 2 * units, tok_rows)
    to_owner = lax.all_to_all(to_owner, "ep", split_axis=0, concat_axis=0, tiled=True)
    shared_whole = lax.all_gather(shared_in, "ep", axis=0, tiled=True)
    shared_scaled = lax.dot_general(
        to_owner.reshape(-1, tok_rows),
        shared_whole,
        (((0,), (0,)), ((), ())),
        preferred_element_type=F32,
    ) * rms

    def to_tokens(row_value):
        token_value = jnp.sum(
            jnp.where(own_hit, row_value.reshape(2, ROWS, 1), 0.0), axis=1
        ).reshape(GROUPS, tok_rows)
        own_blocks = lax.dynamic_slice_in_dim(to_path, GROUPS * tp, GROUPS, 0)
        return jnp.dot(own_blocks.T, token_value, precision=HIGHEST)

    shared_inner = lax.dynamic_update_slice_in_dim(
        jnp.zeros((EXPERTS, tok_rows), F32),
        jnp.sum(gate_cot_s * gate_s + up_cot_s * up_s, axis=1),
        8 * tp,
        0,
    )
    sums = jnp.stack([to_tokens(row_cot), to_tokens(row_inner) + shared_inner], axis=1)
    sums = tp_sum(lax.all_to_all(sums, "ep", split_axis=0, concat_axis=0, tiled=True))
    weight_cot = sums[:, 0].T
    chosen_cot = picks * (
        ROUTE_SCALE
        * (
            weight_cot / chosen_total
            - jnp.sum(weight_cot * chosen, axis=1, keepdims=True) / (chosen_total * chosen_total)
        )
    )
    logit_cot = chosen_cot * scores * (1.0 - scores)
    grad_router = ep_sum(jnp.dot(logit_cot.T, normed.astype(F32), precision=HIGHEST)).T
    router_cot = jnp.dot(logit_cot, router_weight.T, precision=HIGHEST)
    inner_sum = jnp.sum(sums[:, 1], axis=0).reshape(tok_rows, 1) * rms + jnp.sum(
        logit_cot * plain_logits, axis=1, keepdims=True
    )

    scaled = (routed_cot + router_cot) * gain + shared_scaled
    input_cot = inv_rms * scaled - wide_in * (inv_rms * inv_rms * inv_rms) * (
        inner_sum / feature_count
    )
    dense_cot = (out_grad.astype(F32) + input_cot).astype(BF16)

    cot_chunks = path_gather(dense_cot)
    gate_t, up_t = dense_gate.T, dense_up.T
    hidden2 = (jax.nn.silu(gate_t.astype(F32)) * up_t.astype(F32)).astype(BF16)
    hidden2_part = dense_hidden(block_of, dense_down, cot_chunks)
    hidden2_cot = tp_scatter(hidden2_part)
    share = 8 * tok_rows
    gate_mine = lax.dynamic_slice_in_dim(gate_t, tp * share, share, 1).astype(F32)
    up_mine = lax.dynamic_slice_in_dim(up_t, tp * share, share, 1).astype(F32)
    grad_gate2, grad_up2 = gate_grads(hidden2_cot, gate_mine, up_mine)
    grad_dense_down = dense_grad(block_of, hidden2, cot_chunks)

    rows_late, cots_late, unused = lax.optimization_barrier((rows_in, both_cots, back[0]))
    cots_late = cots_late.reshape(GROUPS * ROWS, -1)
    units_r = w_gate.shape[1]

    def rows_dot(left, right):
        return lax.dot_general(
            left, right, (((0,), (0,)), ((), ())), preferred_element_type=F32
        ).astype(BF16)[None]

    return (
        grad_gate2.astype(BF16).T,
        grad_up2.astype(BF16).T,
        grad_dense_down,
        rows_dot(rows_late, cots_late[:, :units_r]),
        rows_dot(rows_late, cots_late[:, units_r:]),
        rows_dot(hidden_all, rows_grad),
        grads_in[:units].T,
        grads_in[units:].T,
        grads_down[:units],
        grad_router,
    )


def solution(mesh):
    in_specs = (
        P("ep", "tp"),
        P("ep", "tp"),
        P("tp"),
        P("tp", None),
        P("ep", None),
        P("ep", "tp", None),
        P("ep", "tp", None),
        P("ep", None, "tp"),
        P("tp", "ep"),
        P("tp", "ep"),
        P("ep", "tp"),
        P(None, "ep"),
        P(None, "ep"),
        P("ep", "tp"),
    )
    out_specs = (
        P("tp", "ep"),
        P("tp", "ep"),
        P("ep", "tp"),
        P("ep", "tp", None),
        P("ep", "tp", None),
        P("ep", None, "tp"),
        P("tp", "ep"),
        P("tp", "ep"),
        P("ep", "tp"),
        P("tp", None),
    )
    return jax.shard_map(local, mesh=mesh, in_specs=in_specs, out_specs=out_specs, check_vma=False)
```

time: 994 us -> 517 us (0.52)
  waiting for transfers between devices: 591 us -> 184 us
  local copies, waits for them, and re-layouts: 150 us -> 33.3 us
  Pallas kernels: 0 us -> 76.7 us
  starting transfers between devices: 37.2 us -> 110 us
  other arithmetic: 67.3 us -> 21.7 us
  matrix products: 83.6 us -> 41.6 us
  blocking collectives: 42.4 us -> 26.1 us
    reduce_scatter x4 -> x0, waiting for transfers between devices: 259 us -> none  [the longest x1 81.1 us: local(): lax.psum_scatter(shared_up_term.astype(jnp.bfloat16), 'ep', scatter_dimen...]
    psum x2 -> x0, waiting for transfers between devices: 184 us -> none  [the longest x1 121 us: local(): lax.psum(up_part.astype(jnp.bfloat16), 'tp').astype(jnp.float32)]
    ppermute x0 -> x54, waiting for transfers between devices: none -> 108 us  [the longest x9 32.8 us: path_gather(): lax.ppermute(joined, 'ep', second_hop(k))]
    pallas_call x0 -> x12, Pallas kernels: none -> 76.7 us  [the longest x2 14.7 us: dispatch(): local_call(functools.partial(dispatch_kernel, scale), jax.ShapeDtypeStruc...]
    all_gather x4 -> x1, waiting for transfers between devices: 71.8 us -> 0.02 us  [local(): shared_whole = lax.all_gather(shared_in, 'ep', axis=0, tiled=True)]
    ppermute x0 -> x54, starting transfers between devices: none -> 70.5 us  [the longest x6 14.6 us: tp_sum(): lax.ppermute(value, 'tp', tp_hop(k))]
    convert_element_type x6 -> x1, local copies, waits for them, and re-layouts: 44.8 us -> 0.01 us  [local(): position = told_path[:, :, 0].astype(jnp.int32)]
    psum x4 -> x0, blocking collectives: 42.4 us -> none  [the longest x1 14.3 us: local(): lax.psum(jnp.dot(normed.astype(jnp.float32), router_weight, precision=hig...]
  transfers between devices with their start and end apart: 15 -> 63, of which waited for: 10 -> 25; matrix products, arithmetic and copies ran while one was open for 22% -> 15% of each run, Pallas kernels for 0% -> 13%
where the time goes in v1:
time: 517 us; the launch traced here: 509 us
  waiting for transfers between devices  184 us (36%)
  starting transfers between devices  110 us (21%)
  Pallas kernels  76.7 us (15%)
  matrix products  41.6 us (8%)
  local copies, waits for them, and re-layouts  33.3 us (6%)
  blocking collectives  26.1 us (5%)
  other arithmetic  21.7 us (4%)
  between operations  15.2 us (3%)
    all_to_all x6, waiting for transfers between devices, tp_exchange(): return lax.all_to_all(parts, 'tp', split_axis=0, concat_axis=0, tiled=True)  70.9 us
    ppermute x9, waiting for transfers between devices, path_gather(): lax.ppermute(joined, 'ep', second_hop(k))  32.8 us
    ppermute x9, waiting for transfers between devices, path_gather(): lax.ppermute(block, 'ep', first_hop(k))  31.9 us
    all_to_all x6, starting transfers between devices, tp_exchange(): return lax.all_to_all(parts, 'tp', split_axis=0, concat_axis=0, tiled=True)  26.4 us
    unnamed x100, local copies, waits for them, and re-layouts  19.5 us
    dot_general x3, matrix products, rows_dot(): lax.dot_general(left, right, (((0,), (0,)), ((), ())), preferred_element_...  17.7 us
    ppermute x5, waiting for transfers between devices, ep_sum(): value = value + lax.ppermute(value, 'ep', pairs)  17.3 us
    all_to_all x1, blocking collectives, tp_exchange(): return lax.all_to_all(parts, 'tp', split_axis=0, concat_axis=0, tiled=True)  15.4 us
  transfers between devices with their start and end apart: 63, of which 25 were waited for; matrix products, arithmetic and copies ran while one was open for 15% of the time, Pallas kernels for 13%

profile of v1, /device:TPU:0, one launch (start us, length us, event | category | flops | bytes accessed | tf_op | source)
XLA Modules:
  0.0 508.5 jit_solution(9416727101193144423)
XLA Ops:
  7.2 4.0 collective-permute-start.7
  12.3 2.2 collective-permute-start.8
  16.5 3.5 collective-permute-done.6.refs_1_
  22.1 3.1 collective-permute-start.11
  26.8 2.7 collective-permute-start.18
  31.2 7.5 %collective-permute-done.18.refs_3_ = bf16[128,1280]{1,0:T(8,128)(2,1)S(1)} collective-permute-done((bf16[128,1280]{1,0:T(8,128)(2,1)}, bf16[128,1280]{1,0:T(8,128)(2,1)S(1)}, u32[]{:S(2)}, u32[]{:S(2)}) %collective-permute-start.18) | collective-permute-done | bytes 327712 | tf_op jit(solution)/shard_map/ppermute | solution.py:79
  40.4 2.7 collective-permute-done.17.refs_2_
  43.1 2.8 collective-permute-start.2
  45.9 6.8 %collective-permute-done.16.refs_1_ = bf16[128,1280]{1,0:T(8,128)(2,1)S(1)} collective-permute-done((bf16[128,1280]{1,0:T(8,128)(2,1)}, bf16[128,1280]{1,0:T(8,128)(2,1)S(1)}, u32[]{:S(2)}, u32[]{:S(2)}) %collective-permute-start.16) | collective-permute-done | bytes 327712 | tf_op jit(solution)/shard_map/ppermute | solution.py:79
  52.7 3.0 collective-permute-start.1
  57.9 3.5 collective-permute-done.11.refs_5_.refs_3_
  61.4 4.1 collective-permute-done.9.refs_3_.refs_1_
  71.3 12.1 %collective-permute-done.21.refs_3_.refs_11_ = bf16[512,1280]{1,0:T(8,128)(2,1)} collective-permute-done((bf16[512,1280]{1,0:T(8,128)(2,1)}, bf16[512,1280]{1,0:T(8,128)(2,1)}, u32[]{:S(2)}, u32[]{:S(2)}) %collective-permute-start.21) | collective-permute-done | bytes 1310752 | tf_op jit(solution)/shard_map/ppermute | solution.py:83
  83.4 2.2 collective-permute-done.20.refs_2_.refs_10_
  88.6 11.0 %collective-permute-done.19.refs_1_.refs_9_ = bf16[512,1280]{1,0:T(8,128)(2,1)} collective-permute-done((bf16[512,1280]{1,0:T(8,128)(2,1)}, bf16[512,1280]{1,0:T(8,128)(2,1)}, u32[]{:S(2)}, u32[]{:S(2)}) %collective-permute-start.19) | collective-permute-done | bytes 1310752 | tf_op jit(solution)/shard_map/ppermute | solution.py:83
  101.0 8.0 %all-to-all-start = ((f32[32,3,128]{2,1,0:T(4,128)}), f32[32,3,128]{2,1,0:T(4,128)}, u32[]{:S(2)}, u32[]{:S(2)}) async-start(f32[32,3,128]{2,1,0:T(4,128)} %copy.58), calls=%async_computation | async-start | bytes 131072 | tf_op jit(solution)/shard_map/all_to_all | solution.py:436
  112.2 4.4 all-to-all-done
  118.9 7.3 %shard_map.216 = bf16[8,144,1280]{2,1,0:T(8,128)(2,1)} custom-call(s32[8,1,512]{2,1,0:T(1,128)S(1)} %compare_select_fusion.slot, bf16[512,1280]{1,0:T(8,128)(2,1)} %shard_map.215.refs_0_.refs_8_, bf16[512,1280]{1,0:T(8,128)(2,1)} %collective-permute-done.19.refs_1_.refs_9_, bf16[512,1280]{1,0:T(8,128)(2,1)} %collective-permute-done.20.refs_2_.refs_10_, ...), custom_call_target="tpu_custom_call" | custom-call | flops 1509949440 | bytes 13434880 | tf_op jit(solution)/shard_map/pallas_call | solution.py:151
  126.2 5.5 %convolution_convert_fusion.4 = bf16[1152,768]{1,0:T(8,128)(2,1)} fusion(bf16[1152,1280]{1,0:T(8,128)(2,1)} %bitcast.164, bf16[1,768,1280]{2,1,0:T(8,128)(2,1)S(1)} %copy-done), kind=kOutput, calls=%fused_computation.8 | convolution fusion | flops 2265808896 | bytes 6684672 | tf_op jit(solution)/shard_map/dot_general | solution.py:472
  131.8 12.8 %shard_map.220 = bf16[32,80,128]{2,1,0:T(8,128)(2,1)S(1)} custom-call(s32[32]{0:T(128)S(1)} %multiply_add_fusion.place, bf16[48,1280]{1,0:T(8,128)(2,1)S(1)} %multiply_convert_fusion.w_in, bf16[32,1280]{1,0:T(8,128)(2,1)S(1)} %concatenate.31.w_out, bf16[512,1280]{1,0:T(8,128)(2,1)S(1)} %shard_map.213.refs_2_.refs_0_, ...), custom_call_target="tpu_custom_call" | custom-call | flops 838860800 | bytes 20971520 | tf_op jit(solution)/shard_map/pallas_call | solution.py:277
  144.6 15.4 %all_to_all.50 = bf16[4,8,80,128]{3,2,1,0:T(8,128)(2,1)} all-to-all(bf16[4,8,80,128]{3,2,1,0:T(8,128)(2,1)S(1)} %bitcast.156), channel_id=1, replica_groups=mesh['ep'=32,'tp'=4] {'tp'}, dimensions={0} | all-to-all | bytes 1310720 | tf_op jit(solution)/shard_map/all_to_all | solution.py:100
  160.0 3.6 all-to-all-start.2
  163.6 4.0 copy.62
  167.6 4.0 copy.63
  171.6 7.4 %shard_map.214 = bf16[8,144,1280]{2,1,0:T(8,128)(2,1)} custom-call(s32[8,1,512]{2,1,0:T(1,128)S(1)} %compare_select_fusion.slot, f32[8,1,512]{2,1,0:T(1,128)S(1)} %bitcast.158, f32[1,1280]{1,0:T(1,128)S(1)} %broadcast_in_dim.161.refs_1_.gain, bf16[512,1280]{1,0:T(8,128)(2,1)S(1)} %shard_map.213.refs_2_.refs_0_, ...), custom_call_target="tpu_custom_call" | custom-call | flops 1509949440 | bytes 13434880 | tf_op jit(solution)/shard_map/pallas_call | solution.py:151
  179.0 8.9 %convolution_convert_fusion = bf16[1152,1536]{1,0:T(8,128)(2,1)} fusion(bf16[1152,1280]{1,0:T(8,128)(2,1)} %bitcast.166, bf16[1280,768]{0,1:T(8,128)(2,1)S(1)} %bitcast.162, bf16[1280,768]{0,1:T(8,128)(2,1)S(1)} %bitcast.159), kind=kOutput, calls=%fused_computation | convolution fusion | flops 4539482112 | bytes 10420224 | tf_op jit(solution)/shard_map/dot_general | solution.py:470
  187.9 4.7 all-to-all-start.1
  197.4 36.2 %all-to-all-done.1.gate_ups = bf16[4,288,1536]{2,1,0:T(8,128)(2,1)} async-done(((bf16[4,288,1536]{2,1,0:T(8,128)(2,1)}), bf16[4,288,1536]{2,1,0:T(8,128)(2,1)}, u32[]{:S(2)}, u32[]{:S(2)}) %all-to-all-start.1) | async-done | bytes 3538976 | tf_op jit(solution)/shard_map/all_to_all | solution.py:100
  233.6 5.9 %shard_map.217 = (bf16[4,288,1536]{2,1,0:T(8,128)(2,1)}, bf16[4,288,768]{2,1,0:T(8,128)(2,1)S(1)}, f32[288,1]{1,0:T(8,128)S(1)}, f32[288,1]{1,0:T(8,128)S(1)}) custom-call(f32[288,1]{1,0:T(8,128)S(1)} %reshape.475.weight, bf16[4,288,1536]{2,1,0:T(8,128)(2,1)} %all-to-all-done.1.gate_ups, bf16[4,288,768]{2,1,0:T(8,128)(2,1)S(1)} %all-to-all-done.2.cots), custom_call_target="tpu_custom_call" | custom-call | flops 8847360 | bytes 10616832 | tf_op jit(solution)/shard_map/pallas_call | solution.py:218
  243.6 10.7 %all_to_all.51 = f32[32,2,128]{2,1,0:T(2,128)S(1)} all-to-all(f32[32,2,128]{2,1,0:T(2,128)S(1)} %copy.65), channel_id=1, replica_groups=mesh['ep'=32,'tp'=4] {'ep'}, dimensions={0} | all-to-all | bytes 65536 | tf_op jit(solution)/shard_map/all_to_all | solution.py:547
  254.3 4.9 all-to-all-start.3
  262.2 3.7 pad_maximum_fusion.weights
  266.7 3.4 collective-permute-start.37
  270.7 31.6 %all-to-all-done.3.cots = bf16[4,288,1536]{2,1,0:T(8,128)(2,1)} async-done(((bf16[4,288,1536]{2,1,0:T(8,128)(2,1)}), bf16[4,288,1536]{2,1,0:T(8,128)(2,1)}, u32[]{:S(2)}, u32[]{:S(2)}) %all-to-all-start.3) | async-done | bytes 3538976 | tf_op jit(solution)/shard_map/all_to_all | solution.py:100
  303.3 4.2 all-to-all-start.6
  307.5 9.3 %shard_map.218 = (bf16[144,1280]{1,0:T(8,128)(2,1)S(1)}, bf16[144,1280]{1,0:T(8,128)(2,1)}, bf16[144,1280]{1,0:T(8,128)(2,1)S(1)}, bf16[144,1280]{1,0:T(8,128)(2...) custom-call(bf16[4,288,1536]{2,1,0:T(8,128)(2,1)} %all-to-all-done.3, ...), custom_call_target="tpu_custom_call" | custom-call | flops 4529848320 | bytes 10420224 | tf_op jit(solution)/shard_map/pallas_call | solution.py:176
  320.5 3.2 collective-permute-start.38
  327.9 4.6 all-to-all-start.7
  332.6 2.8 collective-permute-start.28
  335.4 3.0 collective-permute-start.29
  339.1 11.7 %collective-permute-done.28.refs_3_ = bf16[144,1280]{1,0:T(8,128)(2,1)S(1)} collective-permute-done((bf16[144,1280]{1,0:T(8,128)(2,1)}, bf16[144,1280]{1,0:T(8,128)(2,1)S(1)}, u32[]{:S(2)}, u32[]{:S(2)}) %collective-permute-start.28) | collective-permute-done | bytes 368672 | tf_op jit(solution)/shard_map/ppermute | solution.py:490
  350.9 5.8 %collective-permute-done.31.refs_6_ = bf16[144,1280]{1,0:T(8,128)(2,1)S(1)} collective-permute-done((bf16[144,1280]{1,0:T(8,128)(2,1)S(1)}, bf16[144,1280]{1,0:T(8,128)(2,1)S(1)}, u32[]{:S(2)}, u32[]{:S(2)}) %collective-permute-start.31) | collective-permute-done | bytes 368672 | tf_op jit(solution)/shard_map/ppermute | solution.py:489
  357.7 6.3 %shard_map.219 = bf16[512,1280]{1,0:T(8,128)(2,1)} custom-call(s32[512,8]{1,0:T(8,128)S(1)} %bitcast.157, bf16[144,1280]{1,0:T(8,128)(2,1)S(1)} %copy-done.20, bf16[144,1280]{1,0:T(8,128)(2,1)} %collective-permute-done.26.refs_1_, bf16[144,1280]{1,0:T(8,128)(2,1)} %collective-permute-done.27.refs_2_, bf16[144,1280]{1,0:T(8,128)(2,1)S(1)} %collective-permute-done.28.refs_3_, ...), custom_call_target="tpu_custom_call" | custom-call | flops 1509949440 | bytes 4259840 | tf_op jit(solution)/shard_map/pallas_call | solution.py:252
  363.9 2.2 fusion.85
  366.2 2.8 collective-permute-start.33
  369.0 2.5 collective-permute-start.34
  373.9 7.2 %collective-permute-done.35 = bf16[128,1280]{1,0:T(8,128)(2,1)} collective-permute-done((bf16[128,1280]{1,0:T(8,128)(2,1)}, bf16[128,1280]{1,0:T(8,128)(2,1)}, u32[]{:S(2)}, u32[]{:S(2)}) %collective-permute-start.35) | collective-permute-done | bytes 327712 | tf_op jit(solution)/shard_map/ppermute | solution.py:494
  381.1 3.5 fusion.27.refs_0_
  388.6 3.1 collective-permute-done.41.refs_3_
  393.5 3.4 collective-permute-done.39.refs_1_
  399.2 7.1 %collective-permute-done.51 = f32[32,1280]{1,0:T(8,128)S(1)} collective-permute-done((f32[32,1280]{1,0:T(8,128)S(1)}, f32[32,1280]{1,0:T(8,128)S(1)}, u32[]{:S(2)}, u32[]{:S(2)}) %collective-permute-start.51) | collective-permute-done | bytes 163872 | tf_op jit(solution)/shard_map/ppermute | solution.py:91
  407.1 4.1 collective-permute-start.52
  413.4 10.5 %shard_map.224 = (bf16[48,1280]{1,0:T(8,128)(2,1)S(1)}, bf16[32,1280]{1,0:T(8,128)(2,1)S(1)}) custom-call(s32[32]{0:T(128)S(1)} %multiply_add_fusion.place, bf16[32,80,128]{2,1,0:T(8,128)(2,1)} %bitcast.56.cots, f32[1,1280]{1,0:T(1,128)S(1)} %broadcast_in_dim.161.refs_1_.gain, bf16[512,1280]{1,0:T(8,128)(2,1)S(1)} %shard_map.213.refs_2_.refs_0_, ...), custom_call_target="tpu_custom_call" | custom-call | flops 838860800 | bytes 20971520 | tf_op jit(solution)/shard_map/pallas_call | solution.py:303
  423.9 8.8 %collective-permute-done.52 = f32[32,1280]{1,0:T(8,128)} collective-permute-done((f32[32,1280]{1,0:T(8,128)}, f32[32,1280]{1,0:T(8,128)}, u32[]{:S(2)}, u32[]{:S(2)}) %collective-permute-start.52) | collective-permute-done | bytes 163872 | tf_op jit(solution)/shard_map/ppermute | solution.py:91
  434.1 4.4 all-to-all-start.9
  438.5 11.6 %collective-permute-start.45 = (bf16[512,1280]{1,0:T(8,128)(2,1)S(1)}, bf16[512,1280]{1,0:T(8,128)(2,1)S(1)}, u32[]{:S(2)}, u32[]{:S(2)}) collective-permute-start(bf16[512,1280]{1,0:T(8,128)(2,1)S(1)} %shard_map.221.refs_0_), channel_id=1, source_target_pairs={{0,4},{4,0},{8,12},{12,8},{16,20},{20,16},{24,28},{28,24},{32,36},... | collective-permute-start | bytes 3932168 | tf_op jit(solution)/shard_map/ppermute | solution.py:84
  452.9 6.5 %fusion.8 = bf16[1,1280,768]{2,1,0:T(8,128)(2,1)} fusion(bf16[1152,1280]{1,0:T(8,128)(2,1)} %bitcast.167, bf16[1152,1536]{1,0:T(8,128)(2,1)} %bitcast.51), kind=kOutput, calls=%fused_computation.18 | convolution fusion | flops 2265907200 | bytes 6684672 | tf_op jit(solution)/shard_map/dot_general | solution.py:585
  462.4 8.4 %shard_map.222 = bf16[4,192,1024]{2,1,0:T(8,128)(2,1)} custom-call(s32[32]{0:T(128)S(1)} %multiply_add_fusion.place, bf16[192,1280]{1,0:T(8,128)(2,1)S(1)} %copy-done.10, bf16[512,1280]{1,0:T(8,128)(2,1)S(1)} %shard_map.221.refs_0_, bf16[512,1280]{1,0:T(8,128)(2,1)} %collective-permute-done.42.refs_1_, bf16[512,1280]{1,0:T(8,128)(2,1)} %collective-permute-done.43.refs_2_, ...), custom_call_target="tpu_custom_call" | custom-call | flops 2013265920 | bytes 10485760 | tf_op jit(solution)/shard_map/pallas_call | solution.py:327
  470.8 4.7 all-to-all-start.8
  475.5 5.6 %fusion.7 = bf16[1,1280,768]{2,1,0:T(8,128)(2,1)} fusion(bf16[1152,1280]{1,0:T(8,128)(2,1)S(1)} %bitcast.168, bf16[1152,1536]{1,0:T(8,128)(2,1)} %bitcast.51), kind=kOutput, calls=%fused_computation.17 | convolution fusion | flops 2265907200 | bytes 6684672 | tf_op jit(solution)/shard_map/dot_general | solution.py:585
  481.1 5.6 %fusion.9 = bf16[1,768,1280]{2,1,0:T(8,128)(2,1)} fusion(bf16[1152,768]{1,0:T(8,128)(2,1)} %bitcast.54, bf16[1152,1280]{1,0:T(8,128)(2,1)S(1)} %bitcast.165), kind=kOutput, calls=%fused_computation.19 | convolution fusion | flops 2265907200 | bytes 6684672 | tf_op jit(solution)/shard_map/dot_general | solution.py:585
  486.8 7.3 %shard_map.223 = bf16[192,1280]{1,0:T(8,128)(2,1)} custom-call(s32[32]{0:T(128)S(1)} %multiply_add_fusion.place, bf16[192,4096]{1,0:T(8,128)(2,1)} %fusion.3.hidden, bf16[512,1280]{1,0:T(8,128)(2,1)S(1)} %copy-done.3, bf16[512,1280]{1,0:T(8,128)(2,1)} %collective-permute-done.42.refs_1_, bf16[512,1280]{1,0:T(8,128)(2,1)} %collective-permute-done.43.refs_2_, ...), custom_call_target="tpu_custom_call" | custom-call | flops 2013265920 | bytes 10485760 | tf_op jit(solution)/shard_map/pallas_call | solution.py:355
  494.1 3.0 all-to-all-done.8
  498.9 2.4 fusion.20
  (269 shorter events, 74.1 us)
Async XLA Ops:
  7.2 119.1 %copy-start = (bf16[1,768,1280]{2,1,0:T(8,128)(2,1)S(1)}, bf16[1,768,1280]{2,1,0:T(8,128)(2,1)}, u32[]{:S(2)}) copy-start(bf16[1,768,1280]{2,1,0:T(8,128)(2,1)} %param.21) | copy-start | bytes 5898244
  7.2 9.3 %collective-permute-start.7 = (bf16[128,1280]{1,0:T(8,128)(2,1)}, bf16[128,1280]{1,0:T(8,128)(2,1)S(1)}, u32[]{:S(2)}, u32[]{:S(2)}) collective-permute-start(bf16[128,1280]{1,0:T(8,128)(2,1)} %refs_0_.1), channel_id=1, source_target_pairs={{0,64},{4,20},{8,72},{12,28},{16,80},{20,4},{24,88},{28,12},{32,96... | collective-permute-start | bytes 983048 | tf_op jit(solution)/shard_map/ppermute | solution.py:79
  11.2 8.8 %collective-permute-start.6 = (bf16[128,1280]{1,0:T(8,128)(2,1)}, bf16[128,1280]{1,0:T(8,128)(2,1)S(1)}, u32[]{:S(2)}, u32[]{:S(2)}) collective-permute-start(bf16[128,1280]{1,0:T(8,128)(2,1)} %refs_0_.1), channel_id=1, source_target_pairs={{0,32},{4,12},{8,40},{12,20},{16,48},{20,28},{24,56},{28,4},{32,64... | collective-permute-start | bytes 983048 | tf_op jit(solution)/shard_map/ppermute | solution.py:79
  12.3 8.8 %collective-permute-start.8 = (bf16[128,1280]{1,0:T(8,128)(2,1)}, bf16[128,1280]{1,0:T(8,128)(2,1)S(1)}, u32[]{:S(2)}, u32[]{:S(2)}) collective-permute-start(bf16[128,1280]{1,0:T(8,128)(2,1)} %refs_0_.1), channel_id=1, source_target_pairs={{0,96},{4,28},{8,104},{12,4},{16,112},{20,12},{24,120},{28,20},{32... | collective-permute-start | bytes 983048 | tf_op jit(solution)/shard_map/ppermute | solution.py:79
  22.1 39.3 %collective-permute-start.11 = (bf16[512,1280]{1,0:T(8,128)(2,1)S(1)}, bf16[512,1280]{1,0:T(8,128)(2,1)}, u32[]{:S(2)}, u32[]{:S(2)}) collective-permute-start(bf16[512,1280]{1,0:T(8,128)(2,1)S(1)} %shard_map.213.refs_2_.refs_0_), channel_id=1, source_target_pairs={{0,24},{4,100},{8,0},{12,108},{16,8},{20,116},{24,16},{28,124},{32... | collective-permute-start | bytes 3932168 | tf_op jit(solution)/shard_map/ppermute | solution.py:83
  25.2 36.2 %collective-permute-start.10 = (bf16[512,1280]{1,0:T(8,128)(2,1)S(1)}, bf16[512,1280]{1,0:T(8,128)(2,1)}, u32[]{:S(2)}, u32[]{:S(2)}) collective-permute-start(bf16[512,1280]{1,0:T(8,128)(2,1)S(1)} %shard_map.213.refs_2_.refs_0_), channel_id=1, source_target_pairs={{0,16},{4,68},{8,24},{12,76},{16,0},{20,84},{24,8},{28,92},{32,48}... | collective-permute-start | bytes 3932168 | tf_op jit(solution)/shard_map/ppermute | solution.py:83
  25.8 39.7 %collective-permute-start.9 = (bf16[512,1280]{1,0:T(8,128)(2,1)S(1)}, bf16[512,1280]{1,0:T(8,128)(2,1)}, u32[]{:S(2)}, u32[]{:S(2)}) collective-permute-start(bf16[512,1280]{1,0:T(8,128)(2,1)S(1)} %shard_map.213.refs_2_.refs_0_), channel_id=1, source_target_pairs={{0,8},{4,36},{8,16},{12,44},{16,24},{20,52},{24,0},{28,60},{32,40}... | collective-permute-start | bytes 3932168 | tf_op jit(solution)/shard_map/ppermute | solution.py:83
  26.8 11.9 %collective-permute-start.18 = (bf16[128,1280]{1,0:T(8,128)(2,1)}, bf16[128,1280]{1,0:T(8,128)(2,1)S(1)}, u32[]{:S(2)}, u32[]{:S(2)}) collective-permute-start(bf16[128,1280]{1,0:T(8,128)(2,1)} %refs_0_.2), channel_id=1, source_target_pairs={{0,96},{4,28},{8,104},{12,4},{16,112},{20,12},{24,120},{28,20},{32... | collective-permute-start | bytes 983048 | tf_op jit(solution)/shard_map/ppermute | solution.py:79
  30.6 12.5 %collective-permute-start.17 = (bf16[128,1280]{1,0:T(8,128)(2,1)}, bf16[128,1280]{1,0:T(8,128)(2,1)S(1)}, u32[]{:S(2)}, u32[]{:S(2)}) collective-permute-start(bf16[128,1280]{1,0:T(8,128)(2,1)} %refs_0_.2), channel_id=1, source_target_pairs={{0,64},{4,20},{8,72},{12,28},{16,80},{20,4},{24,88},{28,12},{32,96... | collective-permute-start | bytes 983048 | tf_op jit(solution)/shard_map/ppermute | solution.py:79
  38.7 14.1 %collective-permute-start.16 = (bf16[128,1280]{1,0:T(8,128)(2,1)}, bf16[128,1280]{1,0:T(8,128)(2,1)S(1)}, u32[]{:S(2)}, u32[]{:S(2)}) collective-permute-start(bf16[128,1280]{1,0:T(8,128)(2,1)} %refs_0_.2), channel_id=1, source_target_pairs={{0,32},{4,12},{8,40},{12,20},{16,48},{20,28},{24,56},{28,4},{32,64... | collective-permute-start | bytes 983048 | tf_op jit(solution)/shard_map/ppermute | solution.py:79
  43.1 26.6 %collective-permute-start.2 = (f32[128,33]{0,1:T(8,128)S(1)}, f32[128,33]{0,1:T(8,128)S(1)}, u32[]{:S(2)}, u32[]{:S(2)}) collective-permute-start(f32[128,33]{0,1:T(8,128)S(1)} %pad_maximum_fusion.3), channel_id=1, source_target_pairs={{0,3},{1,0},{2,1},{3,2},{4,7},{5,4},{6,5},{7,6},{8,11},{9,8},{10,9... | collective-permute-start | bytes 50696 | tf_op jit(solution)/shard_map/ppermute | solution.py:96
  52.7 18.6 %collective-permute-start.1 = (f32[128,33]{0,1:T(8,128)S(1)}, f32[128,33]{0,1:T(8,128)S(1)}, u32[]{:S(2)}, u32[]{:S(2)}) collective-permute-start(f32[128,33]{0,1:T(8,128)S(1)} %pad_maximum_fusion.3), channel_id=1, source_target_pairs={{0,2},{1,3},{2,0},{3,1},{4,6},{5,7},{6,4},{7,5},{8,10},{9,11},{10,... | collective-permute-start | bytes 50696 | tf_op jit(solution)/shard_map/ppermute | solution.py:96
  65.5 17.9 %collective-permute-start.21 = (bf16[512,1280]{1,0:T(8,128)(2,1)}, bf16[512,1280]{1,0:T(8,128)(2,1)}, u32[]{:S(2)}, u32[]{:S(2)}) collective-permute-start(bf16[512,1280]{1,0:T(8,128)(2,1)} %shard_map.215.refs_0_.refs_8_), channel_id=1, source_target_pairs={{0,24},{4,100},{8,0},{12,108},{16,8},{20,116},{24,16},{28,124},{32... | collective-permute-start | bytes 3932168 | tf_op jit(solution)/shard_map/ppermute | solution.py:83
  66.1 19.5 %collective-permute-start.20 = (bf16[512,1280]{1,0:T(8,128)(2,1)}, bf16[512,1280]{1,0:T(8,128)(2,1)}, u32[]{:S(2)}, u32[]{:S(2)}) collective-permute-start(bf16[512,1280]{1,0:T(8,128)(2,1)} %shard_map.215.refs_0_.refs_8_), channel_id=1, source_target_pairs={{0,16},{4,68},{8,24},{12,76},{16,0},{20,84},{24,8},{28,92},{32,48}... | collective-permute-start | bytes 3932168 | tf_op jit(solution)/shard_map/ppermute | solution.py:83
  68.2 31.4 %collective-permute-start.19 = (bf16[512,1280]{1,0:T(8,128)(2,1)}, bf16[512,1280]{1,0:T(8,128)(2,1)}, u32[]{:S(2)}, u32[]{:S(2)}) collective-permute-start(bf16[512,1280]{1,0:T(8,128)(2,1)} %shard_map.215.refs_0_.refs_8_), channel_id=1, source_target_pairs={{0,8},{4,36},{8,16},{12,44},{16,24},{20,52},{24,0},{28,60},{32,40}... | collective-permute-start | bytes 3932168 | tf_op jit(solution)/shard_map/ppermute | solution.py:83
  69.7 18.2 %collective-permute-start = (f32[128,33]{0,1:T(8,128)S(1)}, f32[128,33]{0,1:T(8,128)S(1)}, u32[]{:S(2)}, u32[]{:S(2)}) collective-permute-start(f32[128,33]{0,1:T(8,128)S(1)} %pad_maximum_fusion.3), channel_id=1, source_target_pairs={{0,1},{1,2},{2,3},{3,0},{4,5},{5,6},{6,7},{7,4},{8,9},{9,10},{10,1... | collective-permute-start | bytes 50696 | tf_op jit(solution)/shard_map/ppermute | solution.py:96
  71.3 39.6 %collective-permute-start.22 = (bf16[512,1280]{1,0:T(8,128)(2,1)}, bf16[512,1280]{1,0:T(8,128)(2,1)}, u32[]{:S(2)}, u32[]{:S(2)}) collective-permute-start(bf16[512,1280]{1,0:T(8,128)(2,1)} %shard_map.215.refs_0_.refs_8_), channel_id=1, source_target_pairs={{0,4},{4,0},{8,12},{12,8},{16,20},{20,16},{24,28},{28,24},{32,36},... | collective-permute-start | bytes 3932168 | tf_op jit(solution)/shard_map/ppermute | solution.py:84
  83.4 27.8 %collective-permute-start.25 = (bf16[512,1280]{1,0:T(8,128)(2,1)}, bf16[512,1280]{1,0:T(8,128)(2,1)}, u32[]{:S(2)}, u32[]{:S(2)}) collective-permute-start(bf16[512,1280]{1,0:T(8,128)(2,1)} %collective-permute-done.21.refs_3_.refs_11_), channel_id=1, source_target_pairs={{0,4},{4,0},{8,12},{12,8},{16,20},{20,16},{24,28},{28,24},{32,36},... | collective-permute-start | bytes 3932168 | tf_op jit(solution)/shard_map/ppermute | solution.py:84
  85.6 25.8 %collective-permute-start.24 = (bf16[512,1280]{1,0:T(8,128)(2,1)}, bf16[512,1280]{1,0:T(8,128)(2,1)}, u32[]{:S(2)}, u32[]{:S(2)}) collective-permute-start(bf16[512,1280]{1,0:T(8,128)(2,1)} %collective-permute-done.20.refs_2_.refs_10_), channel_id=1, source_target_pairs={{0,4},{4,0},{8,12},{12,8},{16,20},{20,16},{24,28},{28,24},{32,36},... | collective-permute-start | bytes 3932168 | tf_op jit(solution)/shard_map/ppermute | solution.py:84
  99.5 19.4 %collective-permute-start.23 = (bf16[512,1280]{1,0:T(8,128)(2,1)}, bf16[512,1280]{1,0:T(8,128)(2,1)}, u32[]{:S(2)}, u32[]{:S(2)}) collective-permute-start(bf16[512,1280]{1,0:T(8,128)(2,1)} %collective-permute-done.19.refs_1_.refs_9_), channel_id=1, source_target_pairs={{0,4},{4,0},{8,12},{12,8},{16,20},{20,16},{24,28},{28,24},{32,36},... | collective-permute-start | bytes 3932168 | tf_op jit(solution)/shard_map/ppermute | solution.py:84
  101.0 15.5 %all-to-all-start = ((f32[32,3,128]{2,1,0:T(4,128)}), f32[32,3,128]{2,1,0:T(4,128)}, u32[]{:S(2)}, u32[]{:S(2)}) async-start(f32[32,3,128]{2,1,0:T(4,128)} %copy.58), calls=%async_computation | async-start | bytes 131072 | tf_op jit(solution)/shard_map/all_to_all | solution.py:436
  110.7 21.1 %collective-permute-start.12 = (bf16[512,1280]{1,0:T(8,128)(2,1)S(1)}, bf16[512,1280]{1,0:T(8,128)(2,1)}, u32[]{:S(2)}, u32[]{:S(2)}) collective-permute-start(bf16[512,1280]{1,0:T(8,128)(2,1)S(1)} %shard_map.213.refs_2_.refs_0_), channel_id=1, source_target_pairs={{0,4},{4,0},{8,12},{12,8},{16,20},{20,16},{24,28},{28,24},{32,36},... | collective-permute-start | bytes 3932168 | tf_op jit(solution)/shard_map/ppermute | solution.py:84
  110.9 20.9 %collective-permute-start.15 = (bf16[512,1280]{1,0:T(8,128)(2,1)}, bf16[512,1280]{1,0:T(8,128)(2,1)}, u32[]{:S(2)}, u32[]{:S(2)}) collective-permute-start(bf16[512,1280]{1,0:T(8,128)(2,1)} %collective-permute-done.11.refs_5_.refs_3_), channel_id=1, source_target_pairs={{0,4},{4,0},{8,12},{12,8},{16,20},{20,16},{24,28},{28,24},{32,36},... | collective-permute-start | bytes 3932168 | tf_op jit(solution)/shard_map/ppermute | solution.py:84
  111.2 20.6 %collective-permute-start.14 = (bf16[512,1280]{1,0:T(8,128)(2,1)}, bf16[512,1280]{1,0:T(8,128)(2,1)}, u32[]{:S(2)}, u32[]{:S(2)}) collective-permute-start(bf16[512,1280]{1,0:T(8,128)(2,1)} %collective-permute-done.10.refs_4_.refs_2_), channel_id=1, source_target_pairs={{0,4},{4,0},{8,12},{12,8},{16,20},{20,16},{24,28},{28,24},{32,36},... | collective-permute-start | bytes 3932168 | tf_op jit(solution)/shard_map/ppermute | solution.py:84
  111.4 20.4 %collective-permute-start.13 = (bf16[512,1280]{1,0:T(8,128)(2,1)}, bf16[512,1280]{1,0:T(8,128)(2,1)}, u32[]{:S(2)}, u32[]{:S(2)}) collective-permute-start(bf16[512,1280]{1,0:T(8,128)(2,1)} %collective-permute-done.9.refs_3_.refs_1_), channel_id=1, source_target_pairs={{0,4},{4,0},{8,12},{12,8},{16,20},{20,16},{24,28},{28,24},{32,36},... | collective-permute-start | bytes 3932168 | tf_op jit(solution)/shard_map/ppermute | solution.py:84
  160.0 27.9 %all-to-all-start.2 = ((bf16[4,288,768]{2,1,0:T(8,128)(2,1)}), bf16[4,288,768]{2,1,0:T(8,128)(2,1)S(1)}, u32[]{:S(2)}, u32[]{:S(2)}) async-start(bf16[4,288,768]{2,1,0:T(8,128)(2,1)} %bitcast.169), calls=%async_computation.2 | async-start | bytes 3538944 | tf_op jit(solution)/shard_map/all_to_all | solution.py:100
  187.9 45.7 %all-to-all-start.1 = ((bf16[4,288,1536]{2,1,0:T(8,128)(2,1)}), bf16[4,288,1536]{2,1,0:T(8,128)(2,1)}, u32[]{:S(2)}, u32[]{:S(2)}) async-start(bf16[4,288,1536]{2,1,0:T(8,128)(2,1)} %bitcast.163), calls=%async_computation.1 | async-start | bytes 7077888 | tf_op jit(solution)/shard_map/all_to_all | solution.py:100
  192.7 179.6 %all-gather.2.cloned.1.call-start = ((), (), s32[]{:S(2)}) async-start(), calls=%async_computation.10 | async-start | bytes 4055040 | tf_op jit(solution)/shard_map/all_gather | solution.py:525
  254.3 48.0 %all-to-all-start.3 = ((bf16[4,288,1536]{2,1,0:T(8,128)(2,1)}), bf16[4,288,1536]{2,1,0:T(8,128)(2,1)}, u32[]{:S(2)}, u32[]{:S(2)}) async-start(bf16[4,288,1536]{2,1,0:T(8,128)(2,1)} %get-tuple-element.47), calls=%async_computation.3 | async-start | bytes 7077888 | tf_op jit(solution)/shard_map/all_to_all | solution.py:100
  259.2 61.3 %collective-permute-start.5 = (f32[32,128]{1,0:T(8,128)S(1)}, f32[32,128]{1,0:T(8,128)}, u32[]{:S(2)}, u32[]{:S(2)}) collective-permute-start(f32[32,128]{1,0:T(8,128)S(1)} %copy-done.40), channel_id=1, source_target_pairs={{0,96},{4,28},{8,104},{12,4},{16,112},{20,12},{24,120},{28,20},{32... | collective-permute-start | bytes 49160 | tf_op jit(solution)/shard_map/ppermute | solution.py:458
  260.4 63.3 %collective-permute-start.4 = (f32[32,128]{1,0:T(8,128)S(1)}, f32[32,128]{1,0:T(8,128)}, u32[]{:S(2)}, u32[]{:S(2)}) collective-permute-start(f32[32,128]{1,0:T(8,128)S(1)} %copy-done.40), channel_id=1, source_target_pairs={{0,64},{4,20},{8,72},{12,28},{16,80},{20,4},{24,88},{28,12},{32,96... | collective-permute-start | bytes 49160 | tf_op jit(solution)/shard_map/ppermute | solution.py:458
  262.0 61.8 %collective-permute-start.3 = (f32[32,128]{1,0:T(8,128)S(1)}, f32[32,128]{1,0:T(8,128)}, u32[]{:S(2)}, u32[]{:S(2)}) collective-permute-start(f32[32,128]{1,0:T(8,128)S(1)} %copy-done.40), channel_id=1, source_target_pairs={{0,32},{4,12},{8,40},{12,20},{16,48},{20,28},{24,56},{28,4},{32,64... | collective-permute-start | bytes 49160 | tf_op jit(solution)/shard_map/ppermute | solution.py:458
  266.7 65.8 %collective-permute-start.37 = (f32[32,2,128]{2,0,1:T(8,128)}, f32[32,2,128]{2,0,1:T(8,128)S(1)}, u32[]{:S(2)}, u32[]{:S(2)}) collective-permute-start(f32[32,2,128]{2,0,1:T(8,128)} %copy.69), channel_id=1, source_target_pairs={{0,2},{1,3},{2,0},{3,1},{4,6},{5,7},{6,4},{7,5},{8,10},{9,11},{10,... | collective-permute-start | bytes 98312 | tf_op jit(solution)/shard_map/ppermute | solution.py:96
  270.1 62.4 %collective-permute-start.36 = (f32[32,2,128]{2,0,1:T(8,128)}, f32[32,2,128]{2,0,1:T(8,128)S(1)}, u32[]{:S(2)}, u32[]{:S(2)}) collective-permute-start(f32[32,2,128]{2,0,1:T(8,128)} %copy.69), channel_id=1, source_target_pairs={{0,1},{1,2},{2,3},{3,0},{4,5},{5,6},{6,7},{7,4},{8,9},{9,10},{10,1... | collective-permute-start | bytes 98312 | tf_op jit(solution)/shard_map/ppermute | solution.py:96
  303.3 22.8 %all-to-all-start.6 = ((bf16[4,8,80,128]{3,2,1,0:T(8,128)(2,1)}), bf16[4,8,80,128]{3,2,1,0:T(8,128)(2,1)}, u32[]{:S(2)}, u32[]{:S(2)}) async-start(bf16[4,8,80,128]{3,2,1,0:T(8,128)(2,1)} %broadcast_in_dim.167), calls=%async_computation.6 | async-start | bytes 1310720 | tf_op jit(solution)/shard_map/all_to_all | solution.py:100
  320.5 12.0 %collective-permute-start.38 = (f32[32,2,128]{2,0,1:T(8,128)}, f32[32,2,128]{2,0,1:T(8,128)S(1)}, u32[]{:S(2)}, u32[]{:S(2)}) collective-permute-start(f32[32,2,128]{2,0,1:T(8,128)} %copy.69), channel_id=1, source_target_pairs={{0,3},{1,0},{2,1},{3,2},{4,7},{5,4},{6,5},{7,6},{8,11},{9,8},{10,9... | collective-permute-start | bytes 98312 | tf_op jit(solution)/shard_map/ppermute | solution.py:96
  323.7 14.7 %collective-permute-start.26 = (bf16[144,1280]{1,0:T(8,128)(2,1)}, bf16[144,1280]{1,0:T(8,128)(2,1)}, u32[]{:S(2)}, u32[]{:S(2)}) collective-permute-start(bf16[144,1280]{1,0:T(8,128)(2,1)} %get-tuple-element.49), channel_id=1, source_target_pairs={{0,4},{4,0},{8,12},{12,8},{16,20},{20,16},{24,28},{28,24},{32,36},... | collective-permute-start | bytes 1105928 | tf_op jit(solution)/shard_map/ppermute | solution.py:490
  323.8 15.3 %collective-permute-start.27 = (bf16[144,1280]{1,0:T(8,128)(2,1)}, bf16[144,1280]{1,0:T(8,128)(2,1)}, u32[]{:S(2)}, u32[]{:S(2)}) collective-permute-start(bf16[144,1280]{1,0:T(8,128)(2,1)} %get-tuple-element.50), channel_id=1, source_target_pairs={{0,24},{4,100},{8,0},{12,108},{16,8},{20,116},{24,16},{28,124},{32... | collective-permute-start | bytes 1105928 | tf_op jit(solution)/shard_map/ppermute | solution.py:489
  327.9 44.3 %all-to-all-start.7 = ((bf16[32,48,128]{2,1,0:T(8,128)(2,1)}), bf16[32,48,128]{2,1,0:T(8,128)(2,1)}, u32[]{:S(2)}, u32[]{:S(2)}) async-start(bf16[32,48,128]{2,1,0:T(8,128)(2,1)} %bitcast.170), calls=%async_computation.7 | async-start | bytes 786432 | tf_op jit(solution)/shard_map/all_to_all | solution.py:524
  332.6 18.3 %collective-permute-start.28 = (bf16[144,1280]{1,0:T(8,128)(2,1)}, bf16[144,1280]{1,0:T(8,128)(2,1)S(1)}, u32[]{:S(2)}, u32[]{:S(2)}) collective-permute-start(bf16[144,1280]{1,0:T(8,128)(2,1)} %copy-done.18), channel_id=1, source_target_pairs={{0,100},{4,24},{8,108},{12,0},{16,116},{20,8},{24,124},{28,16},{32... | collective-permute-start | bytes 1105928 | tf_op jit(solution)/shard_map/ppermute | solution.py:490
  335.4 15.5 %collective-permute-start.29 = (bf16[144,1280]{1,0:T(8,128)(2,1)S(1)}, bf16[144,1280]{1,0:T(8,128)(2,1)S(1)}, u32[]{:S(2)}, u32[]{:S(2)}) collective-permute-start(bf16[144,1280]{1,0:T(8,128)(2,1)S(1)} %copy-done.17), channel_id=1, source_target_pairs={{0,16},{4,68},{8,24},{12,76},{16,0},{20,84},{24,8},{28,92},{32,48}... | collective-permute-start | bytes 1105928 | tf_op jit(solution)/shard_map/ppermute | solution.py:489
  338.4 12.5 %collective-permute-start.30 = (bf16[144,1280]{1,0:T(8,128)(2,1)S(1)}, bf16[144,1280]{1,0:T(8,128)(2,1)S(1)}, u32[]{:S(2)}, u32[]{:S(2)}) collective-permute-start(bf16[144,1280]{1,0:T(8,128)(2,1)S(1)} %copy-done.15), channel_id=1, source_target_pairs={{0,68},{4,16},{8,76},{12,24},{16,84},{20,0},{24,92},{28,8},{32,100... | collective-permute-start | bytes 1105928 | tf_op jit(solution)/shard_map/ppermute | solution.py:490
  338.5 18.2 %collective-permute-start.31 = (bf16[144,1280]{1,0:T(8,128)(2,1)S(1)}, bf16[144,1280]{1,0:T(8,128)(2,1)S(1)}, u32[]{:S(2)}, u32[]{:S(2)}) collective-permute-start(bf16[144,1280]{1,0:T(8,128)(2,1)S(1)} %get-tuple-element.54), channel_id=1, source_target_pairs={{0,8},{4,36},{8,16},{12,44},{16,24},{20,52},{24,0},{28,60},{32,40}... | collective-permute-start | bytes 1105928 | tf_op jit(solution)/shard_map/ppermute | solution.py:489
  339.0 17.6 %collective-permute-start.32 = (bf16[144,1280]{1,0:T(8,128)(2,1)S(1)}, bf16[144,1280]{1,0:T(8,128)(2,1)S(1)}, u32[]{:S(2)}, u32[]{:S(2)}) collective-permute-start(bf16[144,1280]{1,0:T(8,128)(2,1)S(1)} %copy-done.13), channel_id=1, source_target_pairs={{0,36},{4,8},{8,44},{12,16},{16,52},{20,24},{24,60},{28,0},{32,68}... | collective-permute-start | bytes 1105928 | tf_op jit(solution)/shard_map/ppermute | solution.py:490
  366.2 7.7 %collective-permute-start.33 = (bf16[128,1280]{1,0:T(8,128)(2,1)}, bf16[128,1280]{1,0:T(8,128)(2,1)S(1)}, u32[]{:S(2)}, u32[]{:S(2)}) collective-permute-start(bf16[128,1280]{1,0:T(8,128)(2,1)} %get-tuple-element.88), channel_id=1, source_target_pairs={{0,96},{4,28},{8,104},{12,4},{16,112},{20,12},{24,120},{28,20},{32... | collective-permute-start | bytes 983048 | tf_op jit(solution)/shard_map/ppermute | solution.py:494
  369.0 12.1 %collective-permute-start.35 = (bf16[128,1280]{1,0:T(8,128)(2,1)}, bf16[128,1280]{1,0:T(8,128)(2,1)}, u32[]{:S(2)}, u32[]{:S(2)}) collective-permute-start(bf16[128,1280]{1,0:T(8,128)(2,1)} %get-tuple-element.89), channel_id=1, source_target_pairs={{0,32},{4,12},{8,40},{12,20},{16,48},{20,28},{24,56},{28,4},{32,64... | collective-permute-start | bytes 983048 | tf_op jit(solution)/shard_map/ppermute | solution.py:494
  369.0 12.1 %collective-permute-start.34 = (bf16[128,1280]{1,0:T(8,128)(2,1)}, bf16[128,1280]{1,0:T(8,128)(2,1)}, u32[]{:S(2)}, u32[]{:S(2)}) collective-permute-start(bf16[128,1280]{1,0:T(8,128)(2,1)} %get-tuple-element.90), channel_id=1, source_target_pairs={{0,64},{4,20},{8,72},{12,28},{16,80},{20,4},{24,88},{28,12},{32,96... | collective-permute-start | bytes 983048 | tf_op jit(solution)/shard_map/ppermute | solution.py:494
  384.6 7.1 %collective-permute-start.41 = (bf16[128,1280]{1,0:T(8,128)(2,1)S(1)}, bf16[128,1280]{1,0:T(8,128)(2,1)S(1)}, u32[]{:S(2)}, u32[]{:S(2)}) collective-permute-start(bf16[128,1280]{1,0:T(8,128)(2,1)S(1)} %fusion.27.refs_0_), channel_id=1, source_target_pairs={{0,96},{4,28},{8,104},{12,4},{16,112},{20,12},{24,120},{28,20},{32... | collective-permute-start | bytes 983048 | tf_op jit(solution)/shard_map/ppermute | solution.py:79
  384.8 8.7 %collective-permute-start.40 = (bf16[128,1280]{1,0:T(8,128)(2,1)S(1)}, bf16[128,1280]{1,0:T(8,128)(2,1)S(1)}, u32[]{:S(2)}, u32[]{:S(2)}) collective-permute-start(bf16[128,1280]{1,0:T(8,128)(2,1)S(1)} %fusion.27.refs_0_), channel_id=1, source_target_pairs={{0,64},{4,20},{8,72},{12,28},{16,80},{20,4},{24,88},{28,12},{32,96... | collective-permute-start | bytes 983048 | tf_op jit(solution)/shard_map/ppermute | solution.py:79
  385.1 11.8 %collective-permute-start.39 = (bf16[128,1280]{1,0:T(8,128)(2,1)S(1)}, bf16[128,1280]{1,0:T(8,128)(2,1)S(1)}, u32[]{:S(2)}, u32[]{:S(2)}) collective-permute-start(bf16[128,1280]{1,0:T(8,128)(2,1)S(1)} %fusion.27.refs_0_), channel_id=1, source_target_pairs={{0,32},{4,12},{8,40},{12,20},{16,48},{20,28},{24,56},{28,4},{32,64... | collective-permute-start | bytes 983048 | tf_op jit(solution)/shard_map/ppermute | solution.py:79
  387.1 1.5 collective-permute-start.49
  388.6 10.6 %collective-permute-start.50 = (f32[32,1280]{1,0:T(8,128)S(1)}, f32[32,1280]{1,0:T(8,128)S(1)}, u32[]{:S(2)}, u32[]{:S(2)}) collective-permute-start(f32[32,1280]{1,0:T(8,128)S(1)} %add.394), channel_id=1, source_target_pairs={{0,8},{4,12},{8,0},{12,4},{16,24},{20,28},{24,16},{28,20},{32,40},... | collective-permute-start | bytes 491528 | tf_op jit(solution)/shard_map/ppermute | solution.py:91
  397.0 53.1 %collective-permute-start.44 = (bf16[512,1280]{1,0:T(8,128)(2,1)S(1)}, bf16[512,1280]{1,0:T(8,128)(2,1)}, u32[]{:S(2)}, u32[]{:S(2)}) collective-permute-start(bf16[512,1280]{1,0:T(8,128)(2,1)S(1)} %shard_map.221.refs_0_), channel_id=1, source_target_pairs={{0,24},{4,100},{8,0},{12,108},{16,8},{20,116},{24,16},{28,124},{32... | collective-permute-start | bytes 3932168 | tf_op jit(solution)/shard_map/ppermute | solution.py:83
  397.7 52.5 %collective-permute-start.43 = (bf16[512,1280]{1,0:T(8,128)(2,1)S(1)}, bf16[512,1280]{1,0:T(8,128)(2,1)}, u32[]{:S(2)}, u32[]{:S(2)}) collective-permute-start(bf16[512,1280]{1,0:T(8,128)(2,1)S(1)} %shard_map.221.refs_0_), channel_id=1, source_target_pairs={{0,16},{4,68},{8,24},{12,76},{16,0},{20,84},{24,8},{28,92},{32,48}... | collective-permute-start | bytes 3932168 | tf_op jit(solution)/shard_map/ppermute | solution.py:83
  398.6 52.0 %collective-permute-start.42 = (bf16[512,1280]{1,0:T(8,128)(2,1)S(1)}, bf16[512,1280]{1,0:T(8,128)(2,1)}, u32[]{:S(2)}, u32[]{:S(2)}) collective-permute-start(bf16[512,1280]{1,0:T(8,128)(2,1)S(1)} %shard_map.221.refs_0_), channel_id=1, source_target_pairs={{0,8},{4,36},{8,16},{12,44},{16,24},{20,52},{24,0},{28,60},{32,40}... | collective-permute-start | bytes 3932168 | tf_op jit(solution)/shard_map/ppermute | solution.py:83
  399.2 7.2 %collective-permute-start.51 = (f32[32,1280]{1,0:T(8,128)S(1)}, f32[32,1280]{1,0:T(8,128)S(1)}, u32[]{:S(2)}, u32[]{:S(2)}) collective-permute-start(f32[32,1280]{1,0:T(8,128)S(1)} %add.395), channel_id=1, source_target_pairs={{0,32},{4,36},{8,40},{12,44},{16,48},{20,52},{24,56},{28,60},{32,0... | collective-permute-start | bytes 491528 | tf_op jit(solution)/shard_map/ppermute | solution.py:91
  407.1 25.7 %collective-permute-start.52 = (f32[32,1280]{1,0:T(8,128)}, f32[32,1280]{1,0:T(8,128)}, u32[]{:S(2)}, u32[]{:S(2)}) collective-permute-start(f32[32,1280]{1,0:T(8,128)} %add.396), channel_id=1, source_target_pairs={{0,16},{4,20},{8,24},{12,28},{16,0},{20,4},{24,8},{28,12},{32,48},... | collective-permute-start | bytes 491528 | tf_op jit(solution)/shard_map/ppermute | solution.py:91
  433.7 18.5 %collective-permute-start.53 = (f32[32,1280]{1,0:T(8,128)S(1)}, f32[32,1280]{1,0:T(8,128)S(1)}, u32[]{:S(2)}, u32[]{:S(2)}) collective-permute-start(f32[32,1280]{1,0:T(8,128)S(1)} %add.397), channel_id=1, source_target_pairs={{0,64},{4,68},{8,72},{12,76},{16,80},{20,84},{24,88},{28,92},{32,9... | collective-permute-start | bytes 491528 | tf_op jit(solution)/shard_map/ppermute | solution.py:91
  434.1 36.7 %all-to-all-start.9 = ((bf16[4,288,768]{2,1,0:T(8,128)(2,1)}), bf16[4,288,768]{2,1,0:T(8,128)(2,1)}, u32[]{:S(2)}, u32[]{:S(2)}) async-start(bf16[4,288,768]{2,1,0:T(8,128)(2,1)} %copy-done.6), calls=%async_computation.9 | async-start | bytes 3538944 | tf_op jit(solution)/shard_map/all_to_all | solution.py:100
  438.5 20.9 %collective-permute-start.45 = (bf16[512,1280]{1,0:T(8,128)(2,1)S(1)}, bf16[512,1280]{1,0:T(8,128)(2,1)S(1)}, u32[]{:S(2)}, u32[]{:S(2)}) collective-permute-start(bf16[512,1280]{1,0:T(8,128)(2,1)S(1)} %shard_map.221.refs_0_), channel_id=1, source_target_pairs={{0,4},{4,0},{8,12},{12,8},{16,20},{20,16},{24,28},{28,24},{32,36},... | collective-permute-start | bytes 3932168 | tf_op jit(solution)/shard_map/ppermute | solution.py:84
  450.1 9.3 %collective-permute-start.48 = (bf16[512,1280]{1,0:T(8,128)(2,1)}, bf16[512,1280]{1,0:T(8,128)(2,1)S(1)}, u32[]{:S(2)}, u32[]{:S(2)}) collective-permute-start(bf16[512,1280]{1,0:T(8,128)(2,1)} %collective-permute-done.44.refs_3_), channel_id=1, source_target_pairs={{0,4},{4,0},{8,12},{12,8},{16,20},{20,16},{24,28},{28,24},{32,36},... | collective-permute-start | bytes 3932168 | tf_op jit(solution)/shard_map/ppermute | solution.py:84
  450.2 9.2 %collective-permute-start.47 = (bf16[512,1280]{1,0:T(8,128)(2,1)}, bf16[512,1280]{1,0:T(8,128)(2,1)S(1)}, u32[]{:S(2)}, u32[]{:S(2)}) collective-permute-start(bf16[512,1280]{1,0:T(8,128)(2,1)} %collective-permute-done.43.refs_2_), channel_id=1, source_target_pairs={{0,4},{4,0},{8,12},{12,8},{16,20},{20,16},{24,28},{28,24},{32,36},... | collective-permute-start | bytes 3932168 | tf_op jit(solution)/shard_map/ppermute | solution.py:84
  450.6 8.8 %collective-permute-start.46 = (bf16[512,1280]{1,0:T(8,128)(2,1)}, bf16[512,1280]{1,0:T(8,128)(2,1)S(1)}, u32[]{:S(2)}, u32[]{:S(2)}) collective-permute-start(bf16[512,1280]{1,0:T(8,128)(2,1)} %collective-permute-done.42.refs_1_), channel_id=1, source_target_pairs={{0,4},{4,0},{8,12},{12,8},{16,20},{20,16},{24,28},{28,24},{32,36},... | collective-permute-start | bytes 3932168 | tf_op jit(solution)/shard_map/ppermute | solution.py:84
  470.8 26.2 %all-to-all-start.8 = ((bf16[4,192,1024]{2,1,0:T(8,128)(2,1)}), bf16[4,192,1024]{2,1,0:T(8,128)(2,1)}, u32[]{:S(2)}, u32[]{:S(2)}) async-start(bf16[4,192,1024]{2,1,0:T(8,128)(2,1)} %shard_map.222), calls=%async_computation.8 | async-start | bytes 3145728 | tf_op jit(solution)/shard_map/all_to_all | solution.py:100
  (47 other events, 647.8 us)
Sparse Core Ops, SparseCore 0:
  195.7 43.9 all-gather.1
